TPU v7x, 128 devices: a whole 4x4x4 slice. The times are simulated.
128 devices in a mesh: ctx: 32 (over z, y, core), head: 4 (over x).
Axes of the slice: x: 4, y: 4, z: 4, core: 2. Of those that a mesh axis runs over, the one named last changes fastest.
Arguments:
- q_nope: bfloat16 [32, 128, 128], P(None, 'head'), may hold values from -6 to 6
- q_rope: bfloat16 [32, 128, 64], P(None, 'head'), may hold values from -256 to 256
- latent_cache: bfloat16 [32, 16384, 512], P(None, 'ctx'), may hold values from -6 to 6
- rope_keys: bfloat16 [32, 16384, 64], P(None, 'ctx'), may hold values from -4 to 4
- lengths: int32 [32], replicated, may hold values from 8192 to 16384, as said below
- w_uk: bfloat16 [128, 128, 512], P('head', None, 'ctx'), may hold values from -0.5 to 0.5
- w_uv: bfloat16 [128, 512, 128], P('head'), may hold values from -1 to 1
- w_out: bfloat16 [16384, 7168], P('head', 'ctx'), may hold values from -0.1875 to 0.1875
Outputs:
- layer_out: bfloat16 [32, 7168], P('head', 'ctx')
Inputs may be any that keep to these rules, and one draw needn't show every extreme that they name: `lengths`: some row has length 16384 and some row has length 8192.
All inputs are finite; a program needn't handle non-finite values.
Results may differ from a plain program's by a relative error of at most 0.008.
Values may be sent and summed in bfloat16 or wider, within the bound.
A program may use at most 128 MiB of HBM per device.

v0:
```python
import jax
import jax.numpy as jnp
from jax import lax
from jax.sharding import PartitionSpec as P


def project_latent(summed, w_uv):
    return jnp.einsum(
        "rhl,hlv->rhv", summed, w_uv.astype(jnp.float32), precision=lax.Precision.HIGHEST
    )


def finish_values(projected, row_total):
    return (projected / row_total[:, :, None]).astype(jnp.bfloat16)


def body(q_nope, q_rope, latent_cache, rope_keys, lengths, w_uk, w_uv, w_out):
    row_count = q_nope.shape[0]
    ctx_len = latent_cache.shape[1]
    ctx_place = lax.axis_index("ctx")
    columns = jnp.einsum("rhn,hnl->rhl", q_nope, w_uk, preferred_element_type=jnp.float32).astype(
        jnp.bfloat16
    )
    q_latent = lax.all_gather(columns, "ctx", axis=2, tiled=True)
    score_scale = (q_nope.shape[2] + q_rope.shape[2]) ** (-0.5)
    scores = (
        jnp.einsum("rhl,rtl->rht", q_latent, latent_cache, preferred_element_type=jnp.float32)
        + jnp.einsum("rhd,rtd->rht", q_rope, rope_keys, preferred_element_type=jnp.float32)
    ) * score_scale
    position = ctx_place * ctx_len + jnp.arange(ctx_len, dtype=jnp.int32)
    in_range = position[None, None, :] < lengths[:, None, None]
    masked = jnp.where(in_range, scores, jnp.float32(-1e30))
    row_peak = lax.pmax(jnp.max(masked, axis=2), "ctx")
    weights = jnp.where(in_range, jnp.exp(masked - row_peak[:, :, None]), jnp.float32(0.0)).astype(
        jnp.bfloat16
    )
    row_total = jnp.sum(weights.astype(jnp.float32), axis=2)
    summed = jnp.einsum("rht,rtl->rhl", weights, latent_cache, preferred_element_type=jnp.float32)
    summed, row_total = (
        lax.psum_scatter(summed, "ctx", scatter_dimension=0, tiled=True),
        lax.psum_scatter(row_total, "ctx", scatter_dimension=0, tiled=True),
    )
    own_values = finish_values(project_latent(summed, w_uv), row_total)
    values = lax.all_gather(own_values, "ctx", axis=0, tiled=True)
    flattened = values.reshape(row_count, -1)
    head_terms = jnp.dot(flattened, w_out, preferred_element_type=jnp.float32)
    return lax.psum_scatter(head_terms, "head", scatter_dimension=0, tiled=True).astype(
        jnp.bfloat16
    )


def solution(mesh):
    return jax.shard_map(
        body,
        mesh=mesh,
        in_specs=(
            P(None, "head", None),
            P(None, "head", None),
            P(None, "ctx", None),
            P(None, "ctx", None),
            P(),
            P("head", None, "ctx"),
            P("head", None, None),
            P("head", "ctx"),
        ),
        out_specs=P("head", "ctx"),
        check_vma=False,
    )
```

profile of v0, /device:TPU:1, one launch (start us, length us, event | category | flops | bytes accessed | tf_op | source)
XLA Modules:
  0.0 396.3 jit_solution(14237651380170666001)
XLA Ops:
  6.5 0.0 copy-start
  6.5 0.0 all-gather.3.cloned.1.call-start
  6.5 1.4 fusion
  8.0 0.8 copy.10
  8.8 0.0 all-gather.3.cloned.1.call-update
  8.8 0.0 reduce-scatter.3.cloned.1.call-start
  8.9 0.7 broadcast_compare_fusion
  9.6 0.0 copy-start.1
  9.6 53.0 %all-gather.3.cloned.1.call-done = bf16[32,32,512]{1,2,0:T(8,128)(2,1)} async-done(((bf16[32,32,16]{1,2,0:T(8,128)(2,1)}), bf16[32,32,512]{1,2,0:T(8,128)(2,1)}) %all-gather.3.cloned.1.call-update) | async-done | bytes 1048592 | tf_op jit(solution)/shard_map/all_gather | solution.py:24
  62.6 10.9 %fusion.7 = f32[32,32,512]{2,1,0:T(8,128)} fusion(bf16[32,32,512]{1,2,0:T(8,128)(2,1)} %all-gather.3.cloned.1.call-done, bf16[32,512,512]{2,1,0:T(8,128)(2,1)} %param.10), kind=kOutput, calls=%fused_computation.15 | convolution fusion | flops 536870912 | bytes 19922944 | tf_op jit(solution)/shard_map/rhl,rtl->rht/dot_general | solution.py:27
  73.5 0.0 copy-done
  73.5 0.0 copy-done.1
  73.5 3.5 fusion.6
  77.0 120.9 %pmax.7 = f32[32,32]{1,0:T(8,128)S(1)} all-reduce(f32[32,32]{1,0:T(8,128)S(1)} %get-tuple-element.5), channel_id=1, replica_groups=mesh['ctx'=32,'head'=4] {'ctx'}, use_global_device_ids=true, to_apply=%region_1.2 | all-reduce | flops 1024 | bytes 8192 | tf_op jit(solution)/shard_map/pmax | solution.py:33
  197.9 10.8 %fusion.2 = f32[32,32,512]{2,1,0:T(8,128)} fusion(bf16[32,512,512]{2,1,0:T(8,128)(2,1)} %param.10, f32[32,32,512]{2,1,0:T(8,128)} %get-tuple-element.6, f32[32,32]{1,0:T(8,128)S(1)} %pmax.7, pred[32,512]{1,0:T(8,128)(4,1)S(1)} %broadcast_compare_fusion), kind=kOutput, calls=%fused_computation.5 | convolution fusion | flops 538443776 | bytes 20992000 | tf_op jit(solution)/shard_map/rht,rtl->rhl/dot_general | solution.py:38
  208.7 0.0 copy-start.2
  208.7 0.0 reduce-scatter.3.cloned.1.call-update
  208.8 0.0 reduce-scatter.5.cloned.1.call-start
  208.8 0.6 copy-done.2
  209.4 0.6 dynamic-slice
  210.0 2.2 convert_reduce_fusion
  212.2 124.0 %all-reduce = f32[32,32]{1,0:T(8,128)S(1)} all-reduce(f32[32,32]{1,0:T(8,128)S(1)} %convert_reduce_fusion), channel_id=4, replica_groups=mesh['ctx'=32,'head'=4] {'ctx'}, use_global_device_ids=true, to_apply=%region_4.5.clone | all-reduce | flops 1024 | bytes 8192
  336.2 0.7 dynamic-slice_bitcast_fusion
  336.8 0.0 reduce-scatter.3.cloned.1.call-done
  336.9 4.0 fusion.3
  340.8 0.1 divide_convert_fusion
  340.9 27.3 %all-gather = bf16[1024,128]{1,0:T(8,128)(2,1)S(1)} all-gather(bf16[32,128]{1,0:T(8,128)(2,1)S(1)} %divide_convert_fusion), channel_id=2, replica_groups=mesh['ctx'=32,'head'=4] {'ctx'}, dimensions={0}, use_global_device_ids=true | all-gather | bytes 270336 | tf_op jit(solution)/shard_map/all_gather | solution.py:44
  368.2 0.1 reshape.48
  368.3 2.8 fusion.8
  371.1 0.0 reduce-scatter.5.cloned.1.call-update
  371.1 17.3 %reduce-scatter.5.cloned.1.call-done = f32[8,224]{1,0:T(8,128)} async-done(((f32[32,224]{1,0:T(8,128)}), f32[8,224]{1,0:T(8,128)}) %reduce-scatter.5.cloned.1.call-update) | async-done | bytes 7184 | tf_op jit(solution)/shard_map/reduce_scatter | solution.py:47
  388.5 1.3 convert_element_type.28
  (1 shorter events, 0.0 us)
Async XLA Ops:
  6.5 67.0 %copy-start = (bf16[32,512,64]{1,2,0:T(8,128)(2,1)S(1)}, bf16[32,512,64]{1,2,0:T(8,128)(2,1)}, u32[]{:S(2)}) copy-start(bf16[32,512,64]{1,2,0:T(8,128)(2,1)} %param.11) | copy-start | bytes 6291460
  6.5 56.1 %all-gather.3.cloned.1.call-start = ((), (), s32[]{:S(2)}) async-start(), calls=%async_computation.2 | async-start | bytes 4325376 | tf_op jit(solution)/shard_map/all_gather | solution.py:24
  8.8 328.0 %reduce-scatter.3.cloned.1.call-start = ((), (), s32[]{:S(2)}) async-start(), calls=%async_computation.3 | async-start | bytes 2162688 | tf_op jit(solution)/shard_map/reduce_scatter | solution.py:40
  9.6 63.9 %copy-start.1 = (bf16[32,32,64]{2,1,0:T(8,128)(2,1)S(1)}, bf16[32,32,64]{2,1,0:T(8,128)(2,1)}, u32[]{:S(2)}) copy-start(bf16[32,32,64]{2,1,0:T(8,128)(2,1)} %param.9) | copy-start | bytes 393220
  208.7 0.7 copy-start.2
  208.8 179.7 %reduce-scatter.5.cloned.1.call-start = ((), (), s32[]{:S(2)}) async-start(), calls=%async_computation.4 | async-start | bytes 40960 | tf_op jit(solution)/shard_map/reduce_scatter | solution.py:47
Sparse Core Ops, SparseCore 0:
  9.5 53.0 all-gather.2
  208.9 78.7 reduce-scatter.2
  371.3 17.1 reduce-scatter.4
where the time goes:
time: 398 us; the launch traced here: 396 us
  blocking collectives  272 us (68%)
  waiting for transfers between devices  70.4 us (18%)
  matrix products  33.3 us (8%)
  between operations  13.2 us (3%)
  other arithmetic  4.34 us (1%)
    unnamed x1, blocking collectives  124 us
    pmax x1, blocking collectives, body(): row_peak = lax.pmax(jnp.max(masked, axis=2), 'ctx')  121 us
    all_gather x1, waiting for transfers between devices, body(): q_latent = lax.all_gather(columns, 'ctx', axis=2, tiled=True)  53 us
    all_gather x1, blocking collectives, body(): values = lax.all_gather(own_values, 'ctx', axis=0, tiled=True)  27.3 us
    reduce_scatter x1, waiting for transfers between devices, body(): lax.psum_scatter(head_terms, 'head', scatter_dimension=0, tiled=True)  17.3 us
    dot_general x1, matrix products, body(): jnp.einsum('rhl,rtl->rht', q_latent, latent_cache, preferred_element_type...  10.9 us
    dot_general x1, matrix products, body(): jnp.einsum('rht,rtl->rhl', weights, latent_cache, preferred_element_type=...  10.8 us
  transfers between devices with their start and end apart: 3, of which 2 were waited for; matrix products, arithmetic and copies ran while one was open for 1% of the time, Pallas kernels for 0%

commit v1 on v0

v1 whole, which is shorter than its diff:
```python
import functools

import jax
import jax.numpy as jnp
from jax import lax
from jax.experimental import pallas as pl
from jax.experimental.pallas import tpu as pltpu
from jax.sharding import PartitionSpec as P

MESH = pl.DeviceIdType.MESH
F32 = jnp.float32
BF16 = jnp.bfloat16


def nt(a, b):
    return lax.dot_general(a, b, (((1,), (1,)), ((), ())), preferred_element_type=F32)


def nn(a, b):
    return jnp.dot(a, b, preferred_element_type=F32)


def kernel(
    lengths, q_nope, q_rope, cache, keys, w_uk, w_uv, w_out, out,
    qn, wk, ybuf, xbuf, qbuf, qs, rbuf, cbuf, kbuf, uv, wo,
    obuf, stat, rsbuf, statbuf, wcol, vmsg, vbuf, vwide, terms, tbuf,
    load_sem, rope_sems, pair_sems, x_sems, q_sems, rs_sems, stat_sems, v_sems, t_sems,
):
    ctx = lax.axis_index("ctx")
    x = lax.axis_index("head")
    z, y, c = ctx // 8, (ctx // 2) % 4, ctx % 2
    twin = ctx + 1 - 2 * c
    scale = (128 + 64) ** (-0.5)

    def sums_to(block):
        zb, yb = block // 4, block % 4
        return (((x + zb) % 4) * 8 + yb * 2 + c, zb)

    def sums_from(source):
        return ((source // 4) * 8 + (source % 4) * 2 + c, (z + 4 - x) % 4)

    def is_me(device):
        return jnp.logical_and(device[0] == ctx, device[1] == x)

    barrier = pltpu.get_barrier_semaphore()

    def greet_plane(k, carry):
        pl.semaphore_signal(barrier, inc=1, device_id=((ctx + k) % 32, x), device_id_type=MESH)
        return carry

    def greet_source(s, carry):
        device = sums_from(s)

        @pl.when(jnp.logical_not(is_me(device)))
        def _():
            pl.semaphore_signal(barrier, inc=1, device_id=device, device_id_type=MESH)

        return carry

    for k in range(1, 4):
        pl.semaphore_signal(barrier, inc=1, device_id=(ctx, (x + k) % 4), device_id_type=MESH)
    lax.fori_loop(1, 32, greet_plane, 0)
    lax.fori_loop(0, 16, greet_source, 0)

    mine, theirs = 8 * x + 4 * c, 8 * x + 4 * (1 - c)
    half = pl.ds(pl.multiple_of(c * 512, 512), 512)
    loads = [
        pltpu.make_async_copy(q_nope, qn, load_sem.at[0]),
        pltpu.make_async_copy(w_uk, wk, load_sem.at[1]),
        pltpu.make_async_copy(cache.at[pl.ds(mine, 4)], cbuf.at[:, half], load_sem.at[2]),
        pltpu.make_async_copy(keys.at[pl.ds(mine, 4)], kbuf.at[:, :, half], load_sem.at[3]),
        pltpu.make_async_copy(w_uv.at[pl.ds(8 * y, 8)], uv, load_sem.at[4]),
        pltpu.make_async_copy(w_out, wo, load_sem.at[5]),
        pltpu.make_async_copy(q_rope.at[pl.ds(mine, 4)], rbuf.at[x], load_sem.at[6]),
    ]
    for load in loads:
        load.start()

    loads[0].wait()
    loads[1].wait()
    row_head = lax.broadcasted_iota(jnp.int32, (512, 128), 0) // 16
    lane_head = lax.broadcasted_iota(jnp.int32, (512, 128), 1) % 32
    own_head = row_head == lane_head
    for t in range(8):
        every = nt(wk[...], qn[pl.ds(128 * t, 128), :])
        kept = jnp.where(own_head, every, 0.0).reshape(32, 16, 128)
        ybuf[t // 2, t % 2] = jnp.sum(kept, axis=0).astype(BF16)

    n_self = jnp.where((z + 4 - x) % 4 == x, 1, 0)
    pl.semaphore_wait(barrier, 3 + 31 + 16 - n_self)

    sends = []
    own_y = pltpu.make_async_copy(ybuf.at[x], xbuf.at[:, x], x_sems.at[1])
    own_y.start()
    for k in range(1, 4):
        to = (x + k) % 4
        copy = pltpu.make_async_remote_copy(
            src_ref=ybuf.at[to], dst_ref=xbuf.at[:, x], send_sem=x_sems.at[0], recv_sem=x_sems.at[1],
            device_id=(ctx, to), device_id_type=MESH,
        )
        copy.start()
    cache_copy = pltpu.make_async_remote_copy(
        src_ref=cache.at[pl.ds(theirs, 4)], dst_ref=cbuf.at[:, half], send_sem=pair_sems.at[0],
        recv_sem=pair_sems.at[1], device_id=(twin, x), device_id_type=MESH,
    )
    cache_copy.start()
    keys_copy = pltpu.make_async_remote_copy(
        src_ref=keys.at[pl.ds(theirs, 4)], dst_ref=kbuf.at[:, :, half], send_sem=pair_sems.at[2],
        recv_sem=pair_sems.at[3], device_id=(twin, x), device_id_type=MESH,
    )
    keys_copy.start()
    rope_copies = []
    for k in range(1, 4):
        to = (x + k) % 4
        copy = pltpu.make_async_remote_copy(
            src_ref=q_rope.at[pl.ds(8 * to + 4 * c, 4)], dst_ref=rbuf.at[x], send_sem=rope_sems.at[0, k - 1],
            recv_sem=rope_sems.at[1, k - 1], device_id=(ctx, to), device_id_type=MESH,
        )
        copy.start()
        rope_copies.append(copy)

    pltpu.make_async_copy(xbuf, xbuf, x_sems.at[1]).wait()
    own_q = pltpu.make_async_copy(xbuf.at[c], qbuf.at[ctx], q_sems.at[1])
    own_q.start()

    def send_q(k, carry):
        to = (ctx + k) % 32
        pltpu.make_async_remote_copy(
            src_ref=xbuf.at[to % 2], dst_ref=qbuf.at[ctx], send_sem=q_sems.at[0], recv_sem=q_sems.at[1],
            device_id=(to, x), device_id_type=MESH,
        ).start()
        return carry

    lax.fori_loop(1, 32, send_q, 0)

    loads[2].wait()
    loads[3].wait()
    loads[6].wait()
    cache_copy.wait_recv()
    keys_copy.wait_recv()
    for copy in rope_copies:
        copy.wait_recv()
    pltpu.make_async_copy(qbuf, qbuf, q_sems.at[1]).wait()
    for g in range(4):
        turned = qbuf[:, g].reshape(512, 128).T
        for i in range(4):
            qs[i, 32 * g:32 * g + 32, :] = turned[32 * i:32 * i + 32, :]

    place = (ctx // 2) * 1024 + lax.broadcasted_iota(jnp.int32, (128, 1024), 1)
    lane = lax.broadcasted_iota(jnp.int32, (128, 128), 1)
    stats = jnp.zeros((128, 128), F32)
    for pair in range(2):
        parts = []
        for i in (2 * pair, 2 * pair + 1):
            block = cbuf[i]
            rope = rbuf[:, i].reshape(128, 64)
            scores = (nt(qs[i], block) + nn(rope, kbuf[i])) * scale
            inside = place < lengths[mine + i]
            scores = jnp.where(inside, scores, -1e30)
            peak = jnp.max(scores, axis=1, keepdims=True)
            weights = jnp.where(inside, jnp.exp(scores - peak), 0.0).astype(BF16)
            total = jnp.sum(weights.astype(F32), axis=1, keepdims=True)
            parts.append(nn(weights, block))
            stats = jnp.where(lane == i, peak, jnp.where(lane == 4 + i, total, stats))
        for b in range(16):
            obuf[b, pair] = jnp.concatenate(
                [parts[0][8 * b:8 * b + 8], parts[1][8 * b:8 * b + 8]], axis=0
            ).astype(BF16)

        def send_sums(b, carry):
            device = sums_to(b)
            own = is_me(device)
            slot = 4 * z + y

            @pl.when(own)
            def _():
                pltpu.make_async_copy(obuf.at[b, pair], rsbuf.at[pair, slot], rs_sems.at[1, pair]).start()

            @pl.when(jnp.logical_not(own))
            def _():
                pltpu.make_async_remote_copy(
                    src_ref=obuf.at[b, pair], dst_ref=rsbuf.at[pair, slot], send_sem=rs_sems.at[0, pair],
                    recv_sem=rs_sems.at[1, pair], device_id=device, device_id_type=MESH,
                ).start()

            return carry

        lax.fori_loop(0, 16, send_sums, 0)

    stat[...] = stats.T[0:8, :]

    def send_stats(b, carry):
        device = sums_to(b)
        own = is_me(device)
        slot = 4 * z + y

        @pl.when(own)
        def _():
            pltpu.make_async_copy(stat, statbuf.at[slot], stat_sems.at[1]).start()

        @pl.when(jnp.logical_not(own))
        def _():
            pltpu.make_async_remote_copy(
                src_ref=stat, dst_ref=statbuf.at[slot], send_sem=stat_sems.at[0], recv_sem=stat_sems.at[1],
                device_id=device, device_id_type=MESH,
            ).start()

        return carry

    lax.fori_loop(0, 16, send_stats, 0)

    pltpu.make_async_copy(statbuf, statbuf, stat_sems.at[1]).wait()
    peaks, totals = statbuf[:, 0:4, :], statbuf[:, 4:8, :]
    factors = jnp.exp(peaks - jnp.max(peaks, axis=0, keepdims=True))
    factors = factors / jnp.sum(factors * totals, axis=0, keepdims=True)
    factors = jnp.concatenate([factors.reshape(64, 128), jnp.zeros((64, 128), F32)], axis=0)
    wcol[...] = factors.T
    own_factors = wcol[pl.ds(pl.multiple_of(8 * (4 * x + y), 8), 8), :]
    summed = []
    for pair in range(2):
        pltpu.make_async_copy(rsbuf.at[pair], rsbuf.at[pair], rs_sems.at[1, pair]).wait()
        acc = [jnp.zeros((8, 512), F32), jnp.zeros((8, 512), F32)]
        for d in range(16):
            chunk = rsbuf[pair, d].astype(F32)
            for i in range(2):
                at = 4 * d + 2 * pair + i
                acc[i] = acc[i] + own_factors[:, at:at + 1] * chunk[8 * i:8 * i + 8]
        summed += acc
    summed = jnp.concatenate(summed, axis=0)
    high = summed.astype(BF16)
    low = (summed - high.astype(F32)).astype(BF16)
    both = jnp.concatenate([high, low], axis=0)
    loads[4].wait()
    own_row = lax.broadcasted_iota(jnp.int32, (32, 128), 0) % 8
    values = jnp.zeros((32, 128), F32)
    for h in range(8):
        product = nn(both, uv[h])
        values = jnp.where(own_row == h, product[0:32] + product[32:64], values)
    vmsg[...] = values.astype(BF16)

    block_of_rows = 2 * ((z + 4 - x) % 4) + c
    own_v = pltpu.make_async_copy(vmsg, vbuf.at[y, block_of_rows], v_sems.at[1])
    own_v.start()

    def send_v(k, carry):
        pltpu.make_async_remote_copy(
            src_ref=vmsg, dst_ref=vbuf.at[y, block_of_rows], send_sem=v_sems.at[0], recv_sem=v_sems.at[1],
            device_id=((ctx + k) % 32, x), device_id_type=MESH,
        ).start()
        return carry

    lax.fori_loop(1, 32, send_v, 0)
    loads[5].wait()
    pltpu.make_async_copy(vbuf, vbuf, v_sems.at[1]).wait()
    head_terms = jnp.zeros((32, 224), F32)
    for yb in range(4):
        vwide[yb] = vbuf[yb].astype(F32).reshape(256, 128)
        for h in range(0, 8, 2):
            rows = jnp.concatenate(
                [vwide[yb, pl.ds(h, 32, stride=8), :], vwide[yb, pl.ds(h + 1, 32, stride=8), :]], axis=1
            ).astype(BF16)
            head = 8 * yb + h
            head_terms = head_terms + nt(rows, wo[:, 128 * head:128 * head + 256])
    for k in range(4):
        terms[k] = jnp.concatenate([head_terms[8 * k:8 * k + 8], jnp.zeros((8, 32), F32)], axis=1)

    term_copies = []
    for k in range(1, 4):
        to = (x + k) % 4
        copy = pltpu.make_async_remote_copy(
            src_ref=terms.at[to], dst_ref=tbuf.at[k - 1], send_sem=t_sems.at[0, k - 1], recv_sem=t_sems.at[1, k - 1],
            device_id=(ctx, to), device_id_type=MESH,
        )
        copy.start()
        term_copies.append(copy)
    result = terms[x]
    for k in range(3):
        term_copies[k].wait_recv()
        result = result + tbuf[k]
    out[...] = result[:, 0:224].astype(BF16)

    for k in range(3):
        term_copies[k].wait_send()
        rope_copies[k].wait_send()
    cache_copy.wait_send()
    keys_copy.wait_send()
    pltpu.make_async_copy(ybuf.at[pl.ds(0, 3)], ybuf.at[pl.ds(0, 3)], x_sems.at[0]).wait()
    pltpu.make_async_copy(qbuf.at[pl.ds(0, 31)], qbuf.at[pl.ds(0, 31)], q_sems.at[0]).wait()
    flat = vbuf.at[0]
    for k in range(3):
        pltpu.make_async_copy(flat, flat, v_sems.at[0]).wait()
    pltpu.make_async_copy(vbuf.at[0, pl.ds(0, 7)], vbuf.at[0, pl.ds(0, 7)], v_sems.at[0]).wait()

    def sent(b, carry):
        @pl.when(jnp.logical_not(is_me(sums_to(b))))
        def _():
            for pair in range(2):
                pltpu.make_async_copy(obuf.at[b, pair], obuf.at[b, pair], rs_sems.at[0, pair]).wait()
            pltpu.make_async_copy(stat, stat, stat_sems.at[0]).wait()

        return carry

    lax.fori_loop(0, 16, sent, 0)


def body(q_nope, q_rope, latent_cache, rope_keys, lengths, w_uk, w_uv, w_out):
    any_spec = pl.BlockSpec(memory_space=pl.ANY)
    dma = pltpu.SemaphoreType.DMA
    return pl.pallas_call(
        kernel,
        out_shape=jax.ShapeDtypeStruct((8, 224), BF16),
        in_specs=[pl.BlockSpec(memory_space=pltpu.SMEM)] + [any_spec] * 7,
        out_specs=pl.BlockSpec(memory_space=pltpu.VMEM),
        scratch_shapes=[
            pltpu.VMEM((1024, 128), BF16),
            pltpu.VMEM((512, 128), BF16),
            pltpu.VMEM((4, 2, 16, 128), BF16),
            pltpu.VMEM((2, 4, 16, 128), BF16),
            pltpu.VMEM((32, 4, 16, 128), BF16),
            pltpu.VMEM((4, 128, 512), BF16),
            pltpu.VMEM((4, 4, 32, 64), BF16),
            pltpu.VMEM((4, 1024, 512), BF16),
            pltpu.VMEM((4, 64, 1024), BF16),
            pltpu.VMEM((8, 512, 128), BF16),
            pltpu.VMEM((224, 4096), BF16),
            pltpu.VMEM((16, 2, 16, 512), BF16),
            pltpu.VMEM((8, 128), F32),
            pltpu.VMEM((2, 16, 16, 512), BF16),
            pltpu.VMEM((16, 8, 128), F32),
            pltpu.VMEM((128, 128), F32),
            pltpu.VMEM((32, 128), BF16),
            pltpu.VMEM((4, 8, 32, 128), BF16),
            pltpu.VMEM((4, 256, 128), F32),
            pltpu.VMEM((4, 8, 256), F32),
            pltpu.VMEM((3, 8, 256), F32),
            dma((7,)), dma((2, 3)), dma((4,)), dma((2,)), dma((2,)), dma((2, 2)), dma((2,)), dma((2,)), dma((2, 3)),
        ],
        compiler_params=pltpu.CompilerParams(
            collective_id=0, has_side_effects=True, vmem_limit_bytes=48 << 20
        ),
    )(
        lengths,
        q_nope.reshape(1024, 128),
        q_rope,
        latent_cache,
        jnp.swapaxes(rope_keys, 1, 2),
        jnp.swapaxes(w_uk, 1, 2).reshape(512, 128),
        w_uv,
        w_out.T,
    )


def solution(mesh):
    return jax.shard_map(
        body,
        mesh=mesh,
        in_specs=(
            P(None, "head", None),
            P(None, "head", None),
            P(None, "ctx", None),
            P(None, "ctx", None),
            P(),
            P("head", None, "ctx"),
            P("head", None, None),
            P("head", "ctx"),
        ),
        out_specs=P("head", "ctx"),
        check_vma=False,
    )
```

time: 398 us -> 52.8 us (0.13)
  blocking collectives: 272 us -> 0 us
  waiting for transfers between devices: 70.4 us -> 0 us
  Pallas kernels: 0 us -> 45.4 us
  matrix products: 33.3 us -> 0 us
  between operations: 13.2 us -> 0.02 us
  local copies, waits for them, and re-layouts: 2.78 us -> 7.14 us
  other arithmetic: 4.34 us -> 0 us
    unnamed x1 -> x0, blocking collectives: 124 us -> none
    pmax x1 -> x0, blocking collectives: 121 us -> none  [body(): row_peak = lax.pmax(jnp.max(masked, axis=2), 'ctx')]
    all_gather x1 -> x0, waiting for transfers between devices: 53 us -> none  [body(): q_latent = lax.all_gather(columns, 'ctx', axis=2, tiled=True)]
    pallas_call x0 -> x1, Pallas kernels: none -> 45.4 us  [body(): pl.pallas_call(kernel, out_shape=jax.ShapeDtypeStruct((8, 224), BF16), in...]
    dot_general x6 -> x0, matrix products: 33.3 us -> none  [the longest x1 10.9 us: body(): jnp.einsum('rhl,rtl->rht', q_latent, latent_cache, preferred_element_type...]
    all_gather x1 -> x0, blocking collectives: 27.3 us -> none  [body(): values = lax.all_gather(own_values, 'ctx', axis=0, tiled=True)]
    reduce_scatter x2 -> x0, waiting for transfers between devices: 17.4 us -> none  [the longest x1 17.3 us: body(): lax.psum_scatter(head_terms, 'head', scatter_dimension=0, tiled=True)]
    unnamed x7 -> x13, local copies, waits for them, and re-layouts: 1.17 us -> 7.14 us
  transfers between devices with their start and end apart: 3 -> 0, of which waited for: 2 -> 0; matrix products, arithmetic and copies ran while one was open for 1% -> 0% of each run, Pallas kernels for 0% -> 0%
where the time goes in v1:
time: 52.8 us; the launch traced here: 52.5 us
  Pallas kernels  45.4 us (86%)
  local copies, waits for them, and re-layouts  7.14 us (14%)
    pallas_call x1, Pallas kernels, body(): pl.pallas_call(kernel, out_shape=jax.ShapeDtypeStruct((8, 224), BF16), in...  45.4 us
    unnamed x13, local copies, waits for them, and re-layouts  7.14 us

profile of v1, /device:TPU:1, one launch (start us, length us, event | category | flops | bytes accessed | tf_op | source)
XLA Modules:
  0.0 52.5 jit_solution(3641884283307130816)
XLA Ops:
  0.0 0.0 copy-start
  0.0 1.6 %copy-done = bf16[32,512,64]{1,2,0:T(8,128)(2,1)S(1)} copy-done((bf16[32,512,64]{1,2,0:T(8,128)(2,1)S(1)}, bf16[32,512,64]{1,2,0:T(8,128)(2,1)}, u32[]{:S(2)}) %copy-start) | copy-done | bytes 2097176
  1.6 0.0 copy-start.1
  1.6 1.5 %copy-done.1 = bf16[4096,224]{0,1:T(8,128)(2,1)S(1)} copy-done((bf16[4096,224]{0,1:T(8,128)(2,1)S(1)}, bf16[4096,224]{0,1:T(8,128)(2,1)}, u32[]{:S(2)}) %copy-start.1) | copy-done | bytes 1835032
  3.1 0.0 copy-start.2
  3.1 0.9 %copy-done.2 = bf16[32,32,128]{2,1,0:T(8,128)(2,1)S(1)} copy-done((bf16[32,32,128]{2,1,0:T(8,128)(2,1)S(1)}, bf16[32,32,128]{2,1,0:T(8,128)(2,1)}, u32[]{:S(2)}) %copy-start.2) | copy-done | bytes 262168
  4.0 0.0 copy-start.3
  4.0 0.9 %copy-done.3 = bf16[32,32,64]{2,1,0:T(8,128)(2,1)S(1)} copy-done((bf16[32,32,64]{2,1,0:T(8,128)(2,1)S(1)}, bf16[32,32,64]{2,1,0:T(8,128)(2,1)}, u32[]{:S(2)}) %copy-start.3) | copy-done | bytes 131096
  5.0 0.0 copy-start.4
  5.0 0.9 %copy-done.4 = bf16[32,128,16]{1,2,0:T(8,128)(2,1)S(1)} copy-done((bf16[32,128,16]{1,2,0:T(8,128)(2,1)S(1)}, bf16[32,128,16]{1,2,0:T(8,128)(2,1)}, u32[]{:S(2)}) %copy-start.4) | copy-done | bytes 131096
  5.9 0.0 copy-start.5
  5.9 0.7 %copy-done.5 = s32[32]{0:T(128)S(1)} copy-done((s32[32]{0:T(128)S(1)}, s32[32]{0:T(128)}, u32[]{:S(2)}) %copy-start.5) | copy-done | bytes 152
  6.6 45.4 %shard_map.82 = bf16[8,224]{1,0:T(8,128)(2,1)S(1)} custom-call(s32[32]{0:T(128)S(1)} %copy-done.5, bf16[1024,128]{1,0:T(8,128)(2,1)S(1)} %bitcast.8, bf16[32,32,64]{2,1,0:T(8,128)(2,1)S(1)} %copy-done.3, bf16[32,512,512]{2,1,0:T(8,128)(2,1)} %cache.1, bf16[32,64,512]{2,1,0:T(8,128)(2,1)S(1)} %bitcast.6, bf16[512,128]{1,0:T(8,128)(2,1)S(1)} %bitcast.9, ...), custom_call_target="tpu_custom_call" | custom-call | tf_op jit(solution)/shard_map/pallas_call | solution.py:309
  51.9 0.6 %copy.10 = bf16[8,224]{1,0:T(8,128)(2,1)} copy(bf16[8,224]{1,0:T(8,128)(2,1)S(1)} %shard_map.82) | data formatting | bytes 7168
Async XLA Ops:
  0.0 1.6 %copy-start = (bf16[32,512,64]{1,2,0:T(8,128)(2,1)S(1)}, bf16[32,512,64]{1,2,0:T(8,128)(2,1)}, u32[]{:S(2)}) copy-start(bf16[32,512,64]{1,2,0:T(8,128)(2,1)} %param.11) | copy-start | bytes 6291460
  1.6 1.5 %copy-start.1 = (bf16[4096,224]{0,1:T(8,128)(2,1)S(1)}, bf16[4096,224]{0,1:T(8,128)(2,1)}, u32[]{:S(2)}) copy-start(bf16[4096,224]{0,1:T(8,128)(2,1)} %param.15) | copy-start | bytes 5505028
  3.1 0.9 %copy-start.2 = (bf16[32,32,128]{2,1,0:T(8,128)(2,1)S(1)}, bf16[32,32,128]{2,1,0:T(8,128)(2,1)}, u32[]{:S(2)}) copy-start(bf16[32,32,128]{2,1,0:T(8,128)(2,1)} %param.8) | copy-start | bytes 786436
  4.0 0.9 %copy-start.3 = (bf16[32,32,64]{2,1,0:T(8,128)(2,1)S(1)}, bf16[32,32,64]{2,1,0:T(8,128)(2,1)}, u32[]{:S(2)}) copy-start(bf16[32,32,64]{2,1,0:T(8,128)(2,1)} %q_rope.1) | copy-start | bytes 393220
  5.0 0.9 %copy-start.4 = (bf16[32,128,16]{1,2,0:T(8,128)(2,1)S(1)}, bf16[32,128,16]{1,2,0:T(8,128)(2,1)}, u32[]{:S(2)}) copy-start(bf16[32,128,16]{1,2,0:T(8,128)(2,1)} %param.13) | copy-start | bytes 393220
  5.9 0.7 %copy-start.5 = (s32[32]{0:T(128)S(1)}, s32[32]{0:T(128)}, u32[]{:S(2)}) copy-start(s32[32]{0:T(128)} %lengths.1) | copy-start | bytes 388

commit v2 on v0

v2 whole, which is shorter than its diff:
```python
import functools

import jax
import jax.numpy as jnp
from jax import lax
from jax.experimental import pallas as pl
from jax.experimental.pallas import tpu as pltpu
from jax.sharding import PartitionSpec as P

MESH = pl.DeviceIdType.MESH
F32 = jnp.float32
BF16 = jnp.bfloat16


def nt(a, b):
    return lax.dot_general(a, b, (((1,), (1,)), ((), ())), preferred_element_type=F32)


def nn(a, b):
    return jnp.dot(a, b, preferred_element_type=F32)


def kernel(
    lengths, q_nope, q_rope, cache, keys, w_uk, w_uv, w_out, out,
    qn, wk, ybuf, xbuf, qbuf, qs, rbuf, cbuf, kbuf, uv, wo,
    obuf, stat, rsbuf, statbuf, wcol, vmsg, vbuf, vwide, terms, tbuf,
    load_sem, rope_sems, pair_sems, x_sems, q_sems, rs_sems, stat_sems, v_sems, t_sems,
):
    ctx = lax.axis_index("ctx")
    x = lax.axis_index("head")
    chip, c = ctx // 2, ctx % 2
    z, y = chip // 4, chip % 4
    twin = ctx + 1 - 2 * c
    scale = (128 + 64) ** (-0.5)

    def remote(src, dst, send_sem, recv_sem, device):
        return pltpu.make_async_remote_copy(
            src_ref=src, dst_ref=dst, send_sem=send_sem, recv_sem=recv_sem, device_id=device, device_id_type=MESH
        )

    def arrived(ref, sem):
        pltpu.make_async_copy(ref, ref, sem).wait()

    across = []
    for k in range(1, 8):
        to_x, to_c = (x + k // 2) % 4, (c + k) % 2
        across.append((to_x, to_c, (2 * chip + to_c, to_x)))
    plane = [(2 * ((chip + k) % 16) + c, x) for k in range(1, 16)]

    loads = [
        pltpu.make_async_copy(q_nope, qn, load_sem.at[0]),
        pltpu.make_async_copy(w_uk, wk, load_sem.at[1]),
    ]
    for load in loads:
        load.start()

    barrier = pltpu.get_barrier_semaphore()
    for device in plane:
        pl.semaphore_signal(barrier, inc=1, device_id=device, device_id_type=MESH)
    for _, _, device in across:
        pl.semaphore_signal(barrier, inc=1, device_id=device, device_id_type=MESH)

    mine, theirs = 8 * x + 4 * c, 8 * x + 4 * (1 - c)
    half = pl.ds(pl.multiple_of(c * 512, 512), 512)
    later = [
        pltpu.make_async_copy(cache.at[pl.ds(mine, 4)], cbuf.at[:, half], load_sem.at[2]),
        pltpu.make_async_copy(keys.at[pl.ds(mine, 4)], kbuf.at[:, :, half], load_sem.at[3]),
        pltpu.make_async_copy(w_uv.at[pl.ds(8 * y, 8)], uv, load_sem.at[4]),
        pltpu.make_async_copy(w_out, wo.at[c], load_sem.at[5]),
        pltpu.make_async_copy(q_rope.at[pl.ds(mine, 4)], rbuf.at[x], load_sem.at[6]),
    ]
    for load in later:
        load.start()
    loads += later

    loads[0].wait()
    loads[1].wait()
    row_head = lax.broadcasted_iota(jnp.int32, (512, 128), 0) // 16
    lane_head = lax.broadcasted_iota(jnp.int32, (512, 128), 1) % 32
    own_head = row_head == lane_head
    for t in range(8):
        every = nt(wk[...], qn[pl.ds(128 * t, 128), :])
        kept = jnp.where(own_head, every, 0.0).reshape(32, 16, 128)
        ybuf[t] = jnp.sum(kept, axis=0).astype(BF16)

    pl.semaphore_wait(barrier, 22)

    slot = 2 * x + c
    for to_x, to_c, device in across:
        remote(ybuf.at[2 * to_x + to_c], xbuf.at[slot], x_sems.at[0], x_sems.at[1], device).start()
    pltpu.make_async_copy(ybuf.at[slot], xbuf.at[slot], x_sems.at[1]).start()
    rope_copies = []
    for k in range(1, 4):
        to = (x + k) % 4
        copy = remote(
            q_rope.at[pl.ds(8 * to + 4 * c, 4)], rbuf.at[x], rope_sems.at[0, k - 1], rope_sems.at[1, k - 1], (ctx, to)
        )
        copy.start()
        rope_copies.append(copy)
    twin_copies = [
        remote(cache.at[pl.ds(theirs, 4)], cbuf.at[:, half], pair_sems.at[0, 0], pair_sems.at[1, 0], (twin, x)),
        remote(keys.at[pl.ds(theirs, 4)], kbuf.at[:, :, half], pair_sems.at[0, 1], pair_sems.at[1, 1], (twin, x)),
        remote(w_out, wo.at[c], pair_sems.at[0, 2], pair_sems.at[1, 2], (twin, x)),
    ]
    twin_copies[0].start()
    twin_copies[1].start()

    arrived(xbuf, x_sems.at[1])
    for device in plane:
        remote(xbuf, qbuf.at[chip], q_sems.at[0], q_sems.at[1], device).start()
    pltpu.make_async_copy(xbuf, qbuf.at[chip], q_sems.at[1]).start()
    twin_copies[2].start()

    loads[2].wait()
    loads[3].wait()
    loads[6].wait()
    twin_copies[0].wait_recv()
    twin_copies[1].wait_recv()
    for copy in rope_copies:
        copy.wait_recv()
    arrived(qbuf, q_sems.at[1])
    for g in range(4):
        turned = qbuf[:, 2 * g:2 * g + 2].reshape(512, 128).T
        for i in range(4):
            qs[i, 32 * g:32 * g + 32, :] = turned[32 * i:32 * i + 32, :]

    place = chip * 1024 + lax.broadcasted_iota(jnp.int32, (128, 1024), 1)
    lane = lax.broadcasted_iota(jnp.int32, (128, 128), 1)
    stats = jnp.zeros((128, 128), F32)
    owners = [(2 * (4 * ((x + b // 4) % 4) + b % 4) + 1 - c, b // 4) for b in range(16)]
    for pair in range(2):
        weighted = []
        for i in (2 * pair, 2 * pair + 1):
            rope = rbuf[:, i].reshape(128, 64)
            scores = (nt(qs[i], cbuf[i]) + nn(rope, kbuf[i])) * scale
            inside = place < lengths[mine + i]
            scores = jnp.where(inside, scores, -1e30)
            peak = jnp.max(scores, axis=1, keepdims=True)
            weights = jnp.where(inside, jnp.exp(scores - peak), 0.0).astype(BF16)
            total = jnp.sum(weights.astype(F32), axis=1, keepdims=True)
            weighted.append(weights)
            stats = jnp.where(lane == i, peak, jnp.where(lane == 4 + i, total, stats))
        if pair == 1:
            stat[...] = stats.T[0:8, :]
            for device in owners:
                remote(stat, statbuf.at[chip], stat_sems.at[0], stat_sems.at[1], device).start()
        parts = [nn(weighted[i], cbuf[2 * pair + i]) for i in range(2)]
        for b in range(16):
            obuf[pair, b] = jnp.concatenate(
                [parts[0][8 * b:8 * b + 8], parts[1][8 * b:8 * b + 8]], axis=0
            ).astype(BF16)
        for b, device in enumerate(owners):
            remote(obuf.at[pair, b], rsbuf.at[pair, chip], rs_sems.at[0, pair], rs_sems.at[1, pair], device).start()

    arrived(statbuf, stat_sems.at[1])
    peaks, totals = statbuf[:, 0:4, :], statbuf[:, 4:8, :]
    factors = jnp.exp(peaks - jnp.max(peaks, axis=0, keepdims=True))
    factors = factors / jnp.sum(factors * totals, axis=0, keepdims=True)
    factors = jnp.concatenate([factors.reshape(64, 128), jnp.zeros((64, 128), F32)], axis=0)
    wcol[...] = factors.T
    own_factors = wcol[pl.ds(pl.multiple_of(8 * (4 * x + y), 8), 8), :]
    summed = []
    for pair in range(2):
        arrived(rsbuf.at[pair], rs_sems.at[1, pair])
        acc = [jnp.zeros((8, 512), F32), jnp.zeros((8, 512), F32)]
        for d in range(16):
            chunk = rsbuf[pair, d].astype(F32)
            for i in range(2):
                at = 4 * d + 2 * pair + i
                acc[i] = acc[i] + own_factors[:, at:at + 1] * chunk[8 * i:8 * i + 8]
        summed += acc
    summed = jnp.concatenate(summed, axis=0)
    high = summed.astype(BF16)
    low = (summed - high.astype(F32)).astype(BF16)
    both = jnp.concatenate([high, low], axis=0)
    loads[4].wait()
    own_row = lax.broadcasted_iota(jnp.int32, (32, 128), 0) % 8
    values = jnp.zeros((32, 128), F32)
    for h in range(8):
        product = nn(both, uv[h])
        values = jnp.where(own_row == h, product[0:32] + product[32:64], values)
    vmsg[...] = values.astype(BF16)

    v_slot = 4 * y + (z + 4 - x) % 4
    for device in plane:
        remote(vmsg, vbuf.at[v_slot], v_sems.at[0], v_sems.at[1], device).start()
    pltpu.make_async_copy(vmsg, vbuf.at[v_slot], v_sems.at[1]).start()
    loads[5].wait()
    twin_copies[2].wait_recv()
    arrived(vbuf, v_sems.at[1])
    head_terms = [jnp.zeros((16, 224), F32)] * 2
    for yb in range(4):
        vwide[yb] = vbuf[4 * yb:4 * yb + 4].astype(F32).reshape(128, 128)
        for h in range(0, 8, 2):
            rows = jnp.concatenate(
                [vwide[yb, pl.ds(h, 16, stride=8), :], vwide[yb, pl.ds(h + 1, 16, stride=8), :]], axis=1
            ).astype(BF16)
            head = 8 * yb + h
            for e in range(2):
                head_terms[e] = head_terms[e] + nt(rows, wo[e, :, 128 * head:128 * head + 256])

    for e in range(2):
        for k in range(4):
            term = head_terms[e][4 * k:4 * k + 4]
            right = jnp.concatenate([term[:, 128:224], jnp.zeros((4, 32), F32)], axis=1)
            terms[2 * k + e] = jnp.concatenate([term[:, 0:128], right], axis=0)
    t_slot = 4 * c + x
    for to_x, to_c, device in across:
        remote(terms.at[2 * to_x + to_c], tbuf.at[t_slot], t_sems.at[0], t_sems.at[1], device).start()
    pltpu.make_async_copy(terms.at[slot], tbuf.at[t_slot], t_sems.at[1]).start()
    arrived(tbuf, t_sems.at[1])
    for e in range(2):
        result = tbuf[4 * e] + tbuf[4 * e + 1] + tbuf[4 * e + 2] + tbuf[4 * e + 3]
        result = jnp.concatenate([result[0:4], result[4:8, 0:96]], axis=1)
        if e == 0:
            lower = result
    out[...] = jnp.concatenate([result, lower], axis=0).astype(BF16)

    for copy in rope_copies + twin_copies:
        copy.wait_send()
    arrived(ybuf.at[pl.ds(0, 7)], x_sems.at[0])
    arrived(qbuf.at[pl.ds(0, 15)], q_sems.at[0])
    arrived(obuf.at[0], rs_sems.at[0, 0])
    arrived(obuf.at[1], rs_sems.at[0, 1])
    arrived(statbuf, stat_sems.at[0])
    arrived(vbuf.at[pl.ds(0, 15)], v_sems.at[0])
    arrived(tbuf.at[pl.ds(0, 7)], t_sems.at[0])


def body(q_nope, q_rope, latent_cache, rope_keys, lengths, w_uk, w_uv, w_out):
    any_spec = pl.BlockSpec(memory_space=pl.ANY)
    dma = pltpu.SemaphoreType.DMA
    return pl.pallas_call(
        kernel,
        out_shape=jax.ShapeDtypeStruct((8, 224), BF16),
        in_specs=[pl.BlockSpec(memory_space=pltpu.SMEM)] + [any_spec] * 7,
        out_specs=pl.BlockSpec(memory_space=pltpu.VMEM),
        scratch_shapes=[
            pltpu.VMEM((1024, 128), BF16),
            pltpu.VMEM((512, 128), BF16),
            pltpu.VMEM((8, 16, 128), BF16),
            pltpu.VMEM((8, 16, 128), BF16),
            pltpu.VMEM((16, 8, 16, 128), BF16),
            pltpu.VMEM((4, 128, 512), BF16),
            pltpu.VMEM((4, 4, 32, 64), BF16),
            pltpu.VMEM((4, 1024, 512), BF16),
            pltpu.VMEM((4, 64, 1024), BF16),
            pltpu.VMEM((8, 512, 128), BF16),
            pltpu.VMEM((2, 224, 4096), BF16),
            pltpu.VMEM((2, 16, 16, 512), BF16),
            pltpu.VMEM((8, 128), F32),
            pltpu.VMEM((2, 16, 16, 512), BF16),
            pltpu.VMEM((16, 8, 128), F32),
            pltpu.VMEM((128, 128), F32),
            pltpu.VMEM((32, 128), BF16),
            pltpu.VMEM((16, 32, 128), BF16),
            pltpu.VMEM((4, 128, 128), F32),
            pltpu.VMEM((8, 8, 128), F32),
            pltpu.VMEM((8, 8, 128), F32),
            dma((7,)), dma((2, 3)), dma((2, 3)), dma((2,)), dma((2,)), dma((2, 2)), dma((2,)), dma((2,)), dma((2,)),
        ],
        compiler_params=pltpu.CompilerParams(
            collective_id=0, has_side_effects=True, vmem_limit_bytes=60 << 20
        ),
    )(
        lengths,
        q_nope.reshape(1024, 128),
        q_rope,
        latent_cache,
        jnp.swapaxes(rope_keys, 1, 2),
        jnp.swapaxes(w_uk, 1, 2).reshape(512, 128),
        w_uv,
        w_out.T,
    )


def solution(mesh):
    return jax.shard_map(
        body,
        mesh=mesh,
        in_specs=(
            P(None, "head", None),
            P(None, "head", None),
            P(None, "ctx", None),
            P(None, "ctx", None),
            P(),
            P("head", None, "ctx"),
            P("head", None, None),
            P("head", "ctx"),
        ),
        out_specs=P("head", "ctx"),
        check_vma=False,
    )
```

time: 398 us -> 46.2 us (0.12)
  blocking collectives: 272 us -> 0 us
  waiting for transfers between devices: 70.4 us -> 0 us
  Pallas kernels: 0 us -> 44.8 us
  matrix products: 33.3 us -> 0 us
  between operations: 13.2 us -> 0.01 us
  other arithmetic: 4.34 us -> 0 us
    unnamed x1 -> x0, blocking collectives: 124 us -> none
    pmax x1 -> x0, blocking collectives: 121 us -> none  [body(): row_peak = lax.pmax(jnp.max(masked, axis=2), 'ctx')]
    all_gather x1 -> x0, waiting for transfers between devices: 53 us -> none  [body(): q_latent = lax.all_gather(columns, 'ctx', axis=2, tiled=True)]
    pallas_call x0 -> x1, Pallas kernels: none -> 44.8 us  [body(): pl.pallas_call(kernel, out_shape=jax.ShapeDtypeStruct((8, 224), BF16), in...]
    dot_general x6 -> x0, matrix products: 33.3 us -> none  [the longest x1 10.9 us: body(): jnp.einsum('rhl,rtl->rht', q_latent, latent_cache, preferred_element_type...]
    all_gather x1 -> x0, blocking collectives: 27.3 us -> none  [body(): values = lax.all_gather(own_values, 'ctx', axis=0, tiled=True)]
    reduce_scatter x2 -> x0, waiting for transfers between devices: 17.4 us -> none  [the longest x1 17.3 us: body(): lax.psum_scatter(head_terms, 'head', scatter_dimension=0, tiled=True)]
  transfers between devices with their start and end apart: 3 -> 0, of which waited for: 2 -> 0; matrix products, arithmetic and copies ran while one was open for 1% -> 0% of each run, Pallas kernels for 0% -> 0%
where the time goes in v2:
time: 46.2 us; the launch traced here: 46 us
  Pallas kernels  44.8 us (97%)
  local copies, waits for them, and re-layouts  1.28 us (3%)
    pallas_call x1, Pallas kernels, body(): pl.pallas_call(kernel, out_shape=jax.ShapeDtypeStruct((8, 224), BF16), in...  44.8 us
    unnamed x1, local copies, waits for them, and re-layouts  1.28 us

profile of v2, /device:TPU:1, one launch (start us, length us, event | category | flops | bytes accessed | tf_op | source)
XLA Modules:
  0.0 46.0 jit_solution(12145013677230812216)
XLA Ops:
  0.0 44.8 %shard_map.82 = bf16[8,224]{1,0:T(8,128)(2,1)} custom-call(s32[32]{0:T(128)} %lengths.1, bf16[1024,128]{1,0:T(8,128)(2,1)} %bitcast.8, bf16[32,32,64]{2,1,0:T(8,128)(2,1)} %q_rope.1, bf16[32,512,512]{2,1,0:T(8,128)(2,1)} %cache.1, bf16[32,64,512]{2,1,0:T(8,128)(2,1)} %bitcast.6, bf16[512,128]{1,0:T(8,128)(2,1)} %bitcast.9, bf16[32,512,128]{2,1,0:T(8,128)(2,1)} %w_uv.1, ...), custom_call_target="tpu_custom_call" | custom-call | tf_op jit(solution)/shard_map/pallas_call | solution.py:233
  44.8 1.3 %copy.10 = bf16[8,224]{1,0:T(8,128)(2,1)} copy(bf16[8,224]{1,0:T(8,128)(2,1)} %shard_map.82) | data formatting | bytes 7168

commit v3 on v2

--- a/solution.py
+++ b/solution.py
@@ -22,9 +22,9 @@
 
 def kernel(
     lengths, q_nope, q_rope, cache, keys, w_uk, w_uv, w_out, out,
-    qn, wk, ybuf, xbuf, qbuf, qs, rbuf, cbuf, kbuf, uv, wo,
+    qn, wk, ybuf, xbuf, ebuf, qbuf, rbuf, cbuf, kbuf, uv, wo,
     obuf, stat, rsbuf, statbuf, wcol, vmsg, vbuf, vwide, terms, tbuf,
-    load_sem, rope_sems, pair_sems, x_sems, q_sems, rs_sems, stat_sems, v_sems, t_sems,
+    load_sem, rope_sems, pair_sems, x_sems, q_sems, rs_sems, stat_sems, v_sems, t_sems, ready,
 ):
     ctx = lax.axis_index("ctx")
     x = lax.axis_index("head")
@@ -45,7 +45,11 @@
     for k in range(1, 8):
         to_x, to_c = (x + k // 2) % 4, (c + k) % 2
         across.append((to_x, to_c, (2 * chip + to_c, to_x)))
-    plane = [(2 * ((chip + k) % 16) + c, x) for k in range(1, 16)]
+    steps = [(a, b) for a in range(4) for b in range(4)]
+    steps.sort(key=lambda s: -(min(s[0], 4 - s[0]) + min(s[1], 4 - s[1])))
+    plane = [(2 * (4 * ((z + a) % 4) + (y + b) % 4) + c, x) for a, b in steps if (a, b) != (0, 0)]
+    along_y = [(2 * (4 * z + (y + b) % 4) + c, x) for b in (2, 1, 3)]
+    along_z = [(2 * (4 * ((z + a) % 4) + y) + c, x) for a in (2, 1, 3)]
 
     loads = [
         pltpu.make_async_copy(q_nope, qn, load_sem.at[0]),
@@ -55,7 +59,7 @@
         load.start()
 
     barrier = pltpu.get_barrier_semaphore()
-    for device in plane:
+    for device in along_y + along_z:
         pl.semaphore_signal(barrier, inc=1, device_id=device, device_id_type=MESH)
     for _, _, device in across:
         pl.semaphore_signal(barrier, inc=1, device_id=device, device_id_type=MESH)
@@ -83,12 +87,14 @@
         kept = jnp.where(own_head, every, 0.0).reshape(32, 16, 128)
         ybuf[t] = jnp.sum(kept, axis=0).astype(BF16)
 
-    pl.semaphore_wait(barrier, 22)
+    pl.semaphore_wait(barrier, 13)
 
     slot = 2 * x + c
     for to_x, to_c, device in across:
         remote(ybuf.at[2 * to_x + to_c], xbuf.at[slot], x_sems.at[0], x_sems.at[1], device).start()
     pltpu.make_async_copy(ybuf.at[slot], xbuf.at[slot], x_sems.at[1]).start()
+    for device in along_y:
+        pl.semaphore_signal(ready, inc=1, device_id=device, device_id_type=MESH)
     rope_copies = []
     for k in range(1, 4):
         to = (x + k) % 4
@@ -106,9 +112,16 @@
     twin_copies[1].start()
 
     arrived(xbuf, x_sems.at[1])
-    for device in plane:
-        remote(xbuf, qbuf.at[chip], q_sems.at[0], q_sems.at[1], device).start()
-    pltpu.make_async_copy(xbuf, qbuf.at[chip], q_sems.at[1]).start()
+    for i in range(4):
+        for e in range(2):
+            ebuf[i // 2, i % 2, e] = jnp.concatenate(
+                [xbuf[2 * g + e, :, 32 * i:32 * i + 32] for g in range(4)], axis=1
+            )
+    pl.semaphore_wait(ready, 3)
+    for pair in range(2):
+        for device in plane:
+            remote(ebuf.at[pair], qbuf.at[pair, chip], q_sems.at[0, pair], q_sems.at[1, pair], device).start()
+        pltpu.make_async_copy(ebuf.at[pair], qbuf.at[pair, chip], q_sems.at[1, pair]).start()
     twin_copies[2].start()
 
     loads[2].wait()
@@ -118,21 +131,21 @@
     twin_copies[1].wait_recv()
     for copy in rope_copies:
         copy.wait_recv()
-    arrived(qbuf, q_sems.at[1])
-    for g in range(4):
-        turned = qbuf[:, 2 * g:2 * g + 2].reshape(512, 128).T
-        for i in range(4):
-            qs[i, 32 * g:32 * g + 32, :] = turned[32 * i:32 * i + 32, :]
 
     place = chip * 1024 + lax.broadcasted_iota(jnp.int32, (128, 1024), 1)
     lane = lax.broadcasted_iota(jnp.int32, (128, 128), 1)
     stats = jnp.zeros((128, 128), F32)
-    owners = [(2 * (4 * ((x + b // 4) % 4) + b % 4) + 1 - c, b // 4) for b in range(16)]
+    owners = []
+    for a, b in steps:
+        to_x, to_y = (x + a) % 4, (y + b) % 4
+        owners.append((4 * to_x + to_y, (2 * (4 * ((x + to_x) % 4) + to_y) + 1 - c, to_x)))
     for pair in range(2):
         weighted = []
+        arrived(qbuf.at[pair], q_sems.at[1, pair])
         for i in (2 * pair, 2 * pair + 1):
             rope = rbuf[:, i].reshape(128, 64)
-            scores = (nt(qs[i], cbuf[i]) + nn(rope, kbuf[i])) * scale
+            query = qbuf[pair, :, i % 2].reshape(512, 128).T
+            scores = (nt(query, cbuf[i]) + nn(rope, kbuf[i])) * scale
             inside = place < lengths[mine + i]
             scores = jnp.where(inside, scores, -1e30)
             peak = jnp.max(scores, axis=1, keepdims=True)
@@ -142,14 +155,14 @@
             stats = jnp.where(lane == i, peak, jnp.where(lane == 4 + i, total, stats))
         if pair == 1:
             stat[...] = stats.T[0:8, :]
-            for device in owners:
+            for _, device in owners:
                 remote(stat, statbuf.at[chip], stat_sems.at[0], stat_sems.at[1], device).start()
         parts = [nn(weighted[i], cbuf[2 * pair + i]) for i in range(2)]
         for b in range(16):
             obuf[pair, b] = jnp.concatenate(
                 [parts[0][8 * b:8 * b + 8], parts[1][8 * b:8 * b + 8]], axis=0
             ).astype(BF16)
-        for b, device in enumerate(owners):
+        for b, device in owners:
             remote(obuf.at[pair, b], rsbuf.at[pair, chip], rs_sems.at[0, pair], rs_sems.at[1, pair], device).start()
 
     arrived(statbuf, stat_sems.at[1])
@@ -219,7 +232,8 @@
     for copy in rope_copies + twin_copies:
         copy.wait_send()
     arrived(ybuf.at[pl.ds(0, 7)], x_sems.at[0])
-    arrived(qbuf.at[pl.ds(0, 15)], q_sems.at[0])
+    for pair in range(2):
+        arrived(qbuf.at[pair, pl.ds(0, 15)], q_sems.at[0, pair])
     arrived(obuf.at[0], rs_sems.at[0, 0])
     arrived(obuf.at[1], rs_sems.at[0, 1])
     arrived(statbuf, stat_sems.at[0])
@@ -240,8 +254,8 @@
             pltpu.VMEM((512, 128), BF16),
             pltpu.VMEM((8, 16, 128), BF16),
             pltpu.VMEM((8, 16, 128), BF16),
-            pltpu.VMEM((16, 8, 16, 128), BF16),
-            pltpu.VMEM((4, 128, 512), BF16),
+            pltpu.VMEM((2, 2, 2, 16, 128), BF16),
+            pltpu.VMEM((2, 16, 2, 2, 16, 128), BF16),
             pltpu.VMEM((4, 4, 32, 64), BF16),
             pltpu.VMEM((4, 1024, 512), BF16),
             pltpu.VMEM((4, 64, 1024), BF16),
@@ -257,7 +271,8 @@
             pltpu.VMEM((4, 128, 128), F32),
             pltpu.VMEM((8, 8, 128), F32),
             pltpu.VMEM((8, 8, 128), F32),
-            dma((7,)), dma((2, 3)), dma((2, 3)), dma((2,)), dma((2,)), dma((2, 2)), dma((2,)), dma((2,)), dma((2,)),
+            dma((7,)), dma((2, 3)), dma((2, 3)), dma((2,)), dma((2, 2)), dma((2, 2)), dma((2,)), dma((2,)), dma((2,)),
+            pltpu.SemaphoreType.REGULAR,
         ],
         compiler_params=pltpu.CompilerParams(
             collective_id=0, has_side_effects=True, vmem_limit_bytes=60 << 20

time: 46.2 us -> 41.7 us (0.903)
  Pallas kernels: 44.8 us -> 40.2 us
    pallas_call x1, Pallas kernels: 44.8 us -> 40.2 us  [body(): pl.pallas_call(kernel, out_shape=jax.ShapeDtypeStruct((8, 224), BF16), in...]
where the time goes in v3:
time: 41.7 us; the launch traced here: 41.5 us
  Pallas kernels  40.2 us (96%)
  local copies, waits for them, and re-layouts  1.28 us (3%)
    pallas_call x1, Pallas kernels, body(): pl.pallas_call(kernel, out_shape=jax.ShapeDtypeStruct((8, 224), BF16), in...  40.2 us
    unnamed x1, local copies, waits for them, and re-layouts  1.28 us

profile of v3, /device:TPU:1, one launch (start us, length us, event | category | flops | bytes accessed | tf_op | source)
XLA Modules:
  0.0 41.5 jit_solution(8871129518285839829)
XLA Ops:
  0.0 40.2 %shard_map.82 = bf16[8,224]{1,0:T(8,128)(2,1)} custom-call(s32[32]{0:T(128)} %lengths.1, bf16[1024,128]{1,0:T(8,128)(2,1)} %bitcast.8, bf16[32,32,64]{2,1,0:T(8,128)(2,1)} %q_rope.1, bf16[32,512,512]{2,1,0:T(8,128)(2,1)} %cache.1, bf16[32,64,512]{2,1,0:T(8,128)(2,1)} %bitcast.6, bf16[512,128]{1,0:T(8,128)(2,1)} %bitcast.9, bf16[32,512,128]{2,1,0:T(8,128)(2,1)} %w_uv.1, ...), custom_call_target="tpu_custom_call" | custom-call | tf_op jit(solution)/shard_map/pallas_call | solution.py:247
  40.2 1.3 %copy.10 = bf16[8,224]{1,0:T(8,128)(2,1)} copy(bf16[8,224]{1,0:T(8,128)(2,1)} %shard_map.82) | data formatting | bytes 7168

commit v4 on v3

--- a/solution.py
+++ b/solution.py
@@ -21,10 +21,10 @@
 
 
 def kernel(
-    lengths, q_nope, q_rope, cache, keys, w_uk, w_uv, w_out, out,
-    qn, wk, ybuf, xbuf, ebuf, qbuf, rbuf, cbuf, kbuf, uv, wo,
+    lengths_in, q_nope, q_rope, cache, keys, w_uk, w_uv, w_out, out,
+    qn, wk, ybuf, xbuf, ebuf, qbuf, rbuf, base, cbuf, kbuf, uv, wo,
     obuf, stat, rsbuf, statbuf, wcol, vmsg, vbuf, vwide, terms, tbuf,
-    load_sem, rope_sems, pair_sems, x_sems, q_sems, rs_sems, stat_sems, v_sems, t_sems, ready,
+    load_sem, rope_sems, pair_sems, x_sems, q_sems, rs_sems, stat_sems, v_sems, t_sems, uv_sems, ready, lengths,
 ):
     ctx = lax.axis_index("ctx")
     x = lax.axis_index("head")
@@ -32,6 +32,7 @@
     z, y = chip // 4, chip % 4
     twin = ctx + 1 - 2 * c
     scale = (128 + 64) ** (-0.5)
+    group = (x + z) % 4
 
     def remote(src, dst, send_sem, recv_sem, device):
         return pltpu.make_async_remote_copy(
@@ -69,13 +70,13 @@
     later = [
         pltpu.make_async_copy(cache.at[pl.ds(mine, 4)], cbuf.at[:, half], load_sem.at[2]),
         pltpu.make_async_copy(keys.at[pl.ds(mine, 4)], kbuf.at[:, :, half], load_sem.at[3]),
-        pltpu.make_async_copy(w_uv.at[pl.ds(8 * y, 8)], uv, load_sem.at[4]),
         pltpu.make_async_copy(w_out, wo.at[c], load_sem.at[5]),
         pltpu.make_async_copy(q_rope.at[pl.ds(mine, 4)], rbuf.at[x], load_sem.at[6]),
+        pltpu.make_async_copy(lengths_in, lengths, load_sem.at[7]),
     ]
     for load in later:
         load.start()
-    loads += later
+    load_cache, load_keys, load_out, load_rope, load_lengths = later
 
     loads[0].wait()
     loads[1].wait()
@@ -110,105 +111,110 @@
     ]
     twin_copies[0].start()
     twin_copies[1].start()
+    heads = w_uv.at[pl.ds(8 * y + 4 * c, 4)]
+    uv_local = pltpu.make_async_copy(heads, uv.at[c], uv_sems.at[1])
+    uv_push = remote(heads, uv.at[c], uv_sems.at[0], uv_sems.at[1], (ctx, (x + 4 - z) % 4))
+    pl.when(z == 0)(uv_local.start)
+    pl.when(z != 0)(uv_push.start)
+    uv_twin = remote(uv.at[c], uv.at[c], uv_sems.at[2], uv_sems.at[3], (twin, x))
 
     arrived(xbuf, x_sems.at[1])
     for i in range(4):
         for e in range(2):
-            ebuf[i // 2, i % 2, e] = jnp.concatenate(
-                [xbuf[2 * g + e, :, 32 * i:32 * i + 32] for g in range(4)], axis=1
-            )
+            ebuf[i, e] = jnp.concatenate([xbuf[2 * g + e, :, 32 * i:32 * i + 32] for g in range(4)], axis=1)
     pl.semaphore_wait(ready, 3)
-    for pair in range(2):
+    for i in range(4):
         for device in plane:
-            remote(ebuf.at[pair], qbuf.at[pair, chip], q_sems.at[0, pair], q_sems.at[1, pair], device).start()
-        pltpu.make_async_copy(ebuf.at[pair], qbuf.at[pair, chip], q_sems.at[1, pair]).start()
+            remote(ebuf.at[i], qbuf.at[i, chip], q_sems.at[0, i], q_sems.at[1, i], device).start()
+        pltpu.make_async_copy(ebuf.at[i], qbuf.at[i, chip], q_sems.at[1, i]).start()
     twin_copies[2].start()
 
-    loads[2].wait()
-    loads[3].wait()
-    loads[6].wait()
-    twin_copies[0].wait_recv()
+    load_keys.wait()
+    load_rope.wait()
+    load_lengths.wait()
     twin_copies[1].wait_recv()
     for copy in rope_copies:
         copy.wait_recv()
-
     place = chip * 1024 + lax.broadcasted_iota(jnp.int32, (128, 1024), 1)
+    for i in range(4):
+        base[i] = jnp.where(place < lengths[mine + i], nn(rbuf[:, i].reshape(128, 64), kbuf[i]), -1e30)
+    load_cache.wait()
+    twin_copies[0].wait_recv()
+
+    def scores_of(i):
+        arrived(qbuf.at[i], q_sems.at[1, i])
+        return nt(qbuf[i].reshape(512, 128).T, cbuf[i]) + base[i]
+
     lane = lax.broadcasted_iota(jnp.int32, (128, 128), 1)
     stats = jnp.zeros((128, 128), F32)
-    owners = []
-    for a, b in steps:
-        to_x, to_y = (x + a) % 4, (y + b) % 4
-        owners.append((4 * to_x + to_y, (2 * (4 * ((x + to_x) % 4) + to_y) + 1 - c, to_x)))
-    for pair in range(2):
-        weighted = []
-        arrived(qbuf.at[pair], q_sems.at[1, pair])
-        for i in (2 * pair, 2 * pair + 1):
-            rope = rbuf[:, i].reshape(128, 64)
-            query = qbuf[pair, :, i % 2].reshape(512, 128).T
-            scores = (nt(query, cbuf[i]) + nn(rope, kbuf[i])) * scale
-            inside = place < lengths[mine + i]
-            scores = jnp.where(inside, scores, -1e30)
-            peak = jnp.max(scores, axis=1, keepdims=True)
-            weights = jnp.where(inside, jnp.exp(scores - peak), 0.0).astype(BF16)
-            total = jnp.sum(weights.astype(F32), axis=1, keepdims=True)
-            weighted.append(weights)
-            stats = jnp.where(lane == i, peak, jnp.where(lane == 4 + i, total, stats))
-        if pair == 1:
+    scores = scores_of(0)
+    for i in range(4):
+        peak = jnp.maximum(jnp.max(scores, axis=1, keepdims=True), -1e29)
+        weights = jnp.exp2((scores - peak) * (scale * 1.4426950408889634))
+        total = jnp.sum(weights, axis=1, keepdims=True)
+        stats = jnp.where(lane == i, peak, jnp.where(lane == 4 + i, total, stats))
+        if i < 3:
+            scores = scores_of(i + 1)
+        else:
             stat[...] = stats.T[0:8, :]
-            for _, device in owners:
+            for device in plane:
                 remote(stat, statbuf.at[chip], stat_sems.at[0], stat_sems.at[1], device).start()
-        parts = [nn(weighted[i], cbuf[2 * pair + i]) for i in range(2)]
-        for b in range(16):
-            obuf[pair, b] = jnp.concatenate(
-                [parts[0][8 * b:8 * b + 8], parts[1][8 * b:8 * b + 8]], axis=0
-            ).astype(BF16)
-        for b, device in owners:
-            remote(obuf.at[pair, b], rsbuf.at[pair, chip], rs_sems.at[0, pair], rs_sems.at[1, pair], device).start()
+            pltpu.make_async_copy(stat, statbuf.at[chip], stat_sems.at[1]).start()
+        part = nn(weights.astype(BF16), cbuf[i]).reshape(16, 8, 512)
+        obuf[i] = jnp.concatenate([part[:, :, 0:256], part[:, :, 256:512]], axis=1).astype(BF16)
+        for a, b in steps:
+            to_z, to_y = (z + a) % 4, (y + b) % 4
+            source = obuf.at[i, 4 * ((x + to_z) % 4) + to_y]
+            if (a, b) == (0, 0):
+                pltpu.make_async_copy(source, rsbuf.at[i, chip], rs_sems.at[1, i]).start()
+            else:
+                device = (2 * (4 * to_z + to_y) + c, x)
+                remote(source, rsbuf.at[i, chip], rs_sems.at[0, i], rs_sems.at[1, i], device).start()
+    uv_local.wait()
+    uv_twin.start()
 
     arrived(statbuf, stat_sems.at[1])
     peaks, totals = statbuf[:, 0:4, :], statbuf[:, 4:8, :]
-    factors = jnp.exp(peaks - jnp.max(peaks, axis=0, keepdims=True))
+    factors = jnp.exp2((peaks - jnp.max(peaks, axis=0, keepdims=True)) * (scale * 1.4426950408889634))
     factors = factors / jnp.sum(factors * totals, axis=0, keepdims=True)
     factors = jnp.concatenate([factors.reshape(64, 128), jnp.zeros((64, 128), F32)], axis=0)
     wcol[...] = factors.T
-    own_factors = wcol[pl.ds(pl.multiple_of(8 * (4 * x + y), 8), 8), :]
+    own_factors = wcol[pl.ds(pl.multiple_of(32 * group + 8 * y, 8), 8), :]
+    own_factors = jnp.concatenate([own_factors, own_factors], axis=0)
     summed = []
-    for pair in range(2):
-        arrived(rsbuf.at[pair], rs_sems.at[1, pair])
-        acc = [jnp.zeros((8, 512), F32), jnp.zeros((8, 512), F32)]
+    for i in range(4):
+        arrived(rsbuf.at[i], rs_sems.at[1, i])
+        acc = jnp.zeros((16, 256), F32)
         for d in range(16):
-            chunk = rsbuf[pair, d].astype(F32)
-            for i in range(2):
-                at = 4 * d + 2 * pair + i
-                acc[i] = acc[i] + own_factors[:, at:at + 1] * chunk[8 * i:8 * i + 8]
-        summed += acc
+            acc = acc + own_factors[:, 4 * d + i:4 * d + i + 1] * rsbuf[i, d].astype(F32)
+        summed.append(jnp.concatenate([acc[0:8], acc[8:16]], axis=1))
     summed = jnp.concatenate(summed, axis=0)
     high = summed.astype(BF16)
     low = (summed - high.astype(F32)).astype(BF16)
     both = jnp.concatenate([high, low], axis=0)
-    loads[4].wait()
+    uv_twin.wait_recv()
     own_row = lax.broadcasted_iota(jnp.int32, (32, 128), 0) % 8
     values = jnp.zeros((32, 128), F32)
-    for h in range(8):
-        product = nn(both, uv[h])
-        values = jnp.where(own_row == h, product[0:32] + product[32:64], values)
+    for h in range(0, 8, 2):
+        product = nn(both, jnp.concatenate([uv[h // 4, h % 4], uv[h // 4, h % 4 + 1]], axis=1))
+        product = product[0:32] + product[32:64]
+        values = jnp.where(own_row == h, product[:, 0:128], jnp.where(own_row == h + 1, product[:, 128:256], values))
     vmsg[...] = values.astype(BF16)
 
-    v_slot = 4 * y + (z + 4 - x) % 4
-    for device in plane:
-        remote(vmsg, vbuf.at[v_slot], v_sems.at[0], v_sems.at[1], device).start()
-    pltpu.make_async_copy(vmsg, vbuf.at[v_slot], v_sems.at[1]).start()
-    loads[5].wait()
+    for a, b in steps:
+        device = (2 * (4 * ((z + a) % 4) + (y + b) % 4) + 1 - c, group)
+        remote(vmsg, vbuf.at[4 * y + x], v_sems.at[0], v_sems.at[1], device).start()
+    load_out.wait()
     twin_copies[2].wait_recv()
     arrived(vbuf, v_sems.at[1])
     head_terms = [jnp.zeros((16, 224), F32)] * 2
-    for yb in range(4):
-        vwide[yb] = vbuf[4 * yb:4 * yb + 4].astype(F32).reshape(128, 128)
+    for k in range(4):
+        vwide[k] = vbuf[4 * k:4 * k + 4].astype(F32).reshape(128, 128)
         for h in range(0, 8, 2):
             rows = jnp.concatenate(
-                [vwide[yb, pl.ds(h, 16, stride=8), :], vwide[yb, pl.ds(h + 1, 16, stride=8), :]], axis=1
+                [vwide[k, pl.ds(h, 16, stride=8), :], vwide[k, pl.ds(h + 1, 16, stride=8), :]], axis=1
             ).astype(BF16)
-            head = 8 * yb + h
+            head = 8 * k + h
             for e in range(2):
                 head_terms[e] = head_terms[e] + nt(rows, wo[e, :, 128 * head:128 * head + 256])
 
@@ -229,15 +235,15 @@
             lower = result
     out[...] = jnp.concatenate([result, lower], axis=0).astype(BF16)
 
-    for copy in rope_copies + twin_copies:
+    for copy in rope_copies + twin_copies + [uv_twin]:
         copy.wait_send()
+    pl.when(z != 0)(uv_push.wait_send)
     arrived(ybuf.at[pl.ds(0, 7)], x_sems.at[0])
-    for pair in range(2):
-        arrived(qbuf.at[pair, pl.ds(0, 15)], q_sems.at[0, pair])
-    arrived(obuf.at[0], rs_sems.at[0, 0])
-    arrived(obuf.at[1], rs_sems.at[0, 1])
-    arrived(statbuf, stat_sems.at[0])
-    arrived(vbuf.at[pl.ds(0, 15)], v_sems.at[0])
+    for i in range(4):
+        arrived(qbuf.at[i, pl.ds(0, 15)], q_sems.at[0, i])
+        arrived(rsbuf.at[i, pl.ds(0, 15)], rs_sems.at[0, i])
+    arrived(statbuf.at[pl.ds(0, 15)], stat_sems.at[0])
+    arrived(vbuf, v_sems.at[0])
     arrived(tbuf.at[pl.ds(0, 7)], t_sems.at[0])
 
 
@@ -247,23 +253,24 @@
     return pl.pallas_call(
         kernel,
         out_shape=jax.ShapeDtypeStruct((8, 224), BF16),
-        in_specs=[pl.BlockSpec(memory_space=pltpu.SMEM)] + [any_spec] * 7,
+        in_specs=[any_spec] * 8,
         out_specs=pl.BlockSpec(memory_space=pltpu.VMEM),
         scratch_shapes=[
             pltpu.VMEM((1024, 128), BF16),
             pltpu.VMEM((512, 128), BF16),
             pltpu.VMEM((8, 16, 128), BF16),
             pltpu.VMEM((8, 16, 128), BF16),
-            pltpu.VMEM((2, 2, 2, 16, 128), BF16),
-            pltpu.VMEM((2, 16, 2, 2, 16, 128), BF16),
+            pltpu.VMEM((4, 2, 16, 128), BF16),
+            pltpu.VMEM((4, 16, 2, 16, 128), BF16),
             pltpu.VMEM((4, 4, 32, 64), BF16),
+            pltpu.VMEM((4, 128, 1024), F32),
             pltpu.VMEM((4, 1024, 512), BF16),
             pltpu.VMEM((4, 64, 1024), BF16),
-            pltpu.VMEM((8, 512, 128), BF16),
+            pltpu.VMEM((2, 4, 512, 128), BF16),
             pltpu.VMEM((2, 224, 4096), BF16),
-            pltpu.VMEM((2, 16, 16, 512), BF16),
+            pltpu.VMEM((4, 16, 16, 256), BF16),
             pltpu.VMEM((8, 128), F32),
-            pltpu.VMEM((2, 16, 16, 512), BF16),
+            pltpu.VMEM((4, 16, 16, 256), BF16),
             pltpu.VMEM((16, 8, 128), F32),
             pltpu.VMEM((128, 128), F32),
             pltpu.VMEM((32, 128), BF16),
@@ -271,8 +278,9 @@
             pltpu.VMEM((4, 128, 128), F32),
             pltpu.VMEM((8, 8, 128), F32),
             pltpu.VMEM((8, 8, 128), F32),
-            dma((7,)), dma((2, 3)), dma((2, 3)), dma((2,)), dma((2, 2)), dma((2, 2)), dma((2,)), dma((2,)), dma((2,)),
+            dma((8,)), dma((2, 3)), dma((2, 3)), dma((2,)), dma((2, 4)), dma((2, 4)), dma((2,)), dma((2,)), dma((2,)), dma((4,)),
             pltpu.SemaphoreType.REGULAR,
+            pltpu.SMEM((32,), jnp.int32),
         ],
         compiler_params=pltpu.CompilerParams(
             collective_id=0, has_side_effects=True, vmem_limit_bytes=60 << 20

time: 41.7 us -> 40.2 us (0.964)
  Pallas kernels: 40.2 us -> 38.8 us
    pallas_call x1, Pallas kernels: 40.2 us -> 38.8 us  [body(): pl.pallas_call(kernel, out_shape=jax.ShapeDtypeStruct((8, 224), BF16), in...]
where the time goes in v4:
time: 40.2 us; the launch traced here: 40.1 us
  Pallas kernels  38.8 us (97%)
  local copies, waits for them, and re-layouts  1.28 us (3%)
    pallas_call x1, Pallas kernels, body(): pl.pallas_call(kernel, out_shape=jax.ShapeDtypeStruct((8, 224), BF16), in...  38.8 us
    unnamed x1, local copies, waits for them, and re-layouts  1.28 us

profile of v4, /device:TPU:1, one launch (start us, length us, event | category | flops | bytes accessed | tf_op | source)
XLA Modules:
  0.0 40.1 jit_solution(11417097292354383826)
XLA Ops:
  0.0 38.8 %shard_map.82 = bf16[8,224]{1,0:T(8,128)(2,1)} custom-call(s32[32]{0:T(128)} %lengths_in.1, bf16[1024,128]{1,0:T(8,128)(2,1)} %bitcast.8, bf16[32,32,64]{2,1,0:T(8,128)(2,1)} %q_rope.1, bf16[32,512,512]{2,1,0:T(8,128)(2,1)} %cache.1, bf16[32,64,512]{2,1,0:T(8,128)(2,1)} %bitcast.6, bf16[512,128]{1,0:T(8,128)(2,1)} %bitcast.9, bf16[32,512,128]{2,1,0:T(8,128)(2,1)} %w_uv.1, ...), custom_call_target="tpu_custom_call" | custom-call | tf_op jit(solution)/shard_map/pallas_call | solution.py:253
  38.8 1.3 %copy.10 = bf16[8,224]{1,0:T(8,128)(2,1)} copy(bf16[8,224]{1,0:T(8,128)(2,1)} %shard_map.82) | data formatting | bytes 7168

commit v5 on v4

--- a/solution.py
+++ b/solution.py
@@ -23,7 +23,7 @@
 def kernel(
     lengths_in, q_nope, q_rope, cache, keys, w_uk, w_uv, w_out, out,
     qn, wk, ybuf, xbuf, ebuf, qbuf, rbuf, base, cbuf, kbuf, uv, wo,
-    obuf, stat, rsbuf, statbuf, wcol, vmsg, vbuf, vwide, terms, tbuf,
+    ctbuf, wot, obuf, stat, rsbuf, statbuf, wcol, vmsg, vbuf, vwide, terms,
     load_sem, rope_sems, pair_sems, x_sems, q_sems, rs_sems, stat_sems, v_sems, t_sems, uv_sems, ready, lengths,
 ):
     ctx = lax.axis_index("ctx")
@@ -67,6 +67,7 @@
 
     mine, theirs = 8 * x + 4 * c, 8 * x + 4 * (1 - c)
     half = pl.ds(pl.multiple_of(c * 512, 512), 512)
+    twin_half = pl.ds(pl.multiple_of((1 - c) * 512, 512), 512)
     later = [
         pltpu.make_async_copy(cache.at[pl.ds(mine, 4)], cbuf.at[:, half], load_sem.at[2]),
         pltpu.make_async_copy(keys.at[pl.ds(mine, 4)], kbuf.at[:, :, half], load_sem.at[3]),
@@ -139,11 +140,15 @@
     for i in range(4):
         base[i] = jnp.where(place < lengths[mine + i], nn(rbuf[:, i].reshape(128, 64), kbuf[i]), -1e30)
     load_cache.wait()
+    for i in range(4):
+        ctbuf[i, :, half] = cbuf[i, half, :].T
     twin_copies[0].wait_recv()
+    for i in range(4):
+        ctbuf[i, :, twin_half] = cbuf[i, twin_half, :].T
 
     def scores_of(i):
         arrived(qbuf.at[i], q_sems.at[1, i])
-        return nt(qbuf[i].reshape(512, 128).T, cbuf[i]) + base[i]
+        return nn(qbuf[i].reshape(512, 128).T, ctbuf[i]) + base[i]
 
     lane = lax.broadcasted_iota(jnp.int32, (128, 128), 1)
     stats = jnp.zeros((128, 128), F32)
@@ -172,6 +177,12 @@
                 remote(source, rsbuf.at[i, chip], rs_sems.at[0, i], rs_sems.at[1, i], device).start()
     uv_local.wait()
     uv_twin.start()
+    load_out.wait()
+    twin_copies[2].wait_recv()
+    for e in range(2):
+        for k in range(4):
+            lanes = slice(1024 * k, 1024 * k + 1024)
+            wot[lanes, 256 * e:256 * e + 256] = jnp.concatenate([wo[e, :, lanes], jnp.zeros((32, 1024), BF16)], axis=0).T
 
     arrived(statbuf, stat_sems.at[1])
     peaks, totals = statbuf[:, 0:4, :], statbuf[:, 4:8, :]
@@ -204,10 +215,8 @@
     for a, b in steps:
         device = (2 * (4 * ((z + a) % 4) + (y + b) % 4) + 1 - c, group)
         remote(vmsg, vbuf.at[4 * y + x], v_sems.at[0], v_sems.at[1], device).start()
-    load_out.wait()
-    twin_copies[2].wait_recv()
     arrived(vbuf, v_sems.at[1])
-    head_terms = [jnp.zeros((16, 224), F32)] * 2
+    head_terms = jnp.zeros((16, 512), F32)
     for k in range(4):
         vwide[k] = vbuf[4 * k:4 * k + 4].astype(F32).reshape(128, 128)
         for h in range(0, 8, 2):
@@ -215,25 +224,18 @@
                 [vwide[k, pl.ds(h, 16, stride=8), :], vwide[k, pl.ds(h + 1, 16, stride=8), :]], axis=1
             ).astype(BF16)
             head = 8 * k + h
-            for e in range(2):
-                head_terms[e] = head_terms[e] + nt(rows, wo[e, :, 128 * head:128 * head + 256])
-
+            head_terms = head_terms + nn(rows, wot[128 * head:128 * head + 256, :])
+
+    rows_c = lax.broadcasted_iota(jnp.int32, (8, 256), 0) // 4 == 1 - c
     for e in range(2):
         for k in range(4):
-            term = head_terms[e][4 * k:4 * k + 4]
-            right = jnp.concatenate([term[:, 128:224], jnp.zeros((4, 32), F32)], axis=1)
-            terms[2 * k + e] = jnp.concatenate([term[:, 0:128], right], axis=0)
+            term = head_terms[4 * k:4 * k + 4, 256 * e:256 * e + 256]
+            terms[2 * k + e] = jnp.where(rows_c, jnp.concatenate([term, term], axis=0), 0.0)
     t_slot = 4 * c + x
     for to_x, to_c, device in across:
-        remote(terms.at[2 * to_x + to_c], tbuf.at[t_slot], t_sems.at[0], t_sems.at[1], device).start()
-    pltpu.make_async_copy(terms.at[slot], tbuf.at[t_slot], t_sems.at[1]).start()
-    arrived(tbuf, t_sems.at[1])
-    for e in range(2):
-        result = tbuf[4 * e] + tbuf[4 * e + 1] + tbuf[4 * e + 2] + tbuf[4 * e + 3]
-        result = jnp.concatenate([result[0:4], result[4:8, 0:96]], axis=1)
-        if e == 0:
-            lower = result
-    out[...] = jnp.concatenate([result, lower], axis=0).astype(BF16)
+        remote(terms.at[2 * to_x + to_c], out.at[t_slot], t_sems.at[0], t_sems.at[1], device).start()
+    pltpu.make_async_copy(terms.at[slot], out.at[t_slot], t_sems.at[1]).start()
+    arrived(out, t_sems.at[1])
 
     for copy in rope_copies + twin_copies + [uv_twin]:
         copy.wait_send()
@@ -244,17 +246,17 @@
         arrived(rsbuf.at[i, pl.ds(0, 15)], rs_sems.at[0, i])
     arrived(statbuf.at[pl.ds(0, 15)], stat_sems.at[0])
     arrived(vbuf, v_sems.at[0])
-    arrived(tbuf.at[pl.ds(0, 7)], t_sems.at[0])
+    arrived(terms.at[pl.ds(0, 7)], t_sems.at[0])
 
 
 def body(q_nope, q_rope, latent_cache, rope_keys, lengths, w_uk, w_uv, w_out):
     any_spec = pl.BlockSpec(memory_space=pl.ANY)
     dma = pltpu.SemaphoreType.DMA
-    return pl.pallas_call(
+    terms = pl.pallas_call(
         kernel,
-        out_shape=jax.ShapeDtypeStruct((8, 224), BF16),
+        out_shape=jax.ShapeDtypeStruct((8, 8, 256), F32),
         in_specs=[any_spec] * 8,
-        out_specs=pl.BlockSpec(memory_space=pltpu.VMEM),
+        out_specs=any_spec,
         scratch_shapes=[
             pltpu.VMEM((1024, 128), BF16),
             pltpu.VMEM((512, 128), BF16),
@@ -268,6 +270,8 @@
             pltpu.VMEM((4, 64, 1024), BF16),
             pltpu.VMEM((2, 4, 512, 128), BF16),
             pltpu.VMEM((2, 224, 4096), BF16),
+            pltpu.VMEM((4, 512, 1024), BF16),
+            pltpu.VMEM((4096, 512), BF16),
             pltpu.VMEM((4, 16, 16, 256), BF16),
             pltpu.VMEM((8, 128), F32),
             pltpu.VMEM((4, 16, 16, 256), BF16),
@@ -276,25 +280,30 @@
             pltpu.VMEM((32, 128), BF16),
             pltpu.VMEM((16, 32, 128), BF16),
             pltpu.VMEM((4, 128, 128), F32),
-            pltpu.VMEM((8, 8, 128), F32),
-            pltpu.VMEM((8, 8, 128), F32),
+            pltpu.VMEM((8, 8, 256), F32),
             dma((8,)), dma((2, 3)), dma((2, 3)), dma((2,)), dma((2, 4)), dma((2, 4)), dma((2,)), dma((2,)), dma((2,)), dma((4,)),
             pltpu.SemaphoreType.REGULAR,
             pltpu.SMEM((32,), jnp.int32),
         ],
         compiler_params=pltpu.CompilerParams(
-            collective_id=0, has_side_effects=True, vmem_limit_bytes=60 << 20
+            collective_id=0, has_side_effects=True, vmem_limit_bytes=48 << 20
         ),
     )(
-        lengths,
-        q_nope.reshape(1024, 128),
-        q_rope,
-        latent_cache,
-        jnp.swapaxes(rope_keys, 1, 2),
-        jnp.swapaxes(w_uk, 1, 2).reshape(512, 128),
-        w_uv,
-        w_out.T,
+        *(
+            pltpu.with_memory_space_constraint(operand, pltpu.HBM)
+            for operand in (
+                lengths,
+                q_nope.reshape(1024, 128),
+                q_rope,
+                latent_cache,
+                jnp.swapaxes(rope_keys, 1, 2),
+                jnp.swapaxes(w_uk, 1, 2).reshape(512, 128),
+                w_uv,
+                w_out.T,
+            )
+        )
     )
+    return jnp.sum(terms, axis=0)[:, 0:224].astype(BF16)
 
 
 def solution(mesh):

time: 40.2 us -> 38.4 us (0.955)
  local copies, waits for them, and re-layouts: 1.28 us -> 0 us
  Pallas kernels: 38.8 us -> 37.7 us
  other arithmetic: 0 us -> 0.6 us
    unnamed x1 -> x0, local copies, waits for them, and re-layouts: 1.28 us -> none
    pallas_call x1, Pallas kernels: 38.8 us -> 37.7 us  [body(): pl.pallas_call(kernel, out_shape=jax.ShapeDtypeStruct((8, 8, 256), F32),...]
    reduce_sum x0 -> x1, other arithmetic: none -> 0.6 us  [body(): return jnp.sum(terms, axis=0)[:, 0:224].astype(BF16)]
where the time goes in v5:
time: 38.4 us; the launch traced here: 38.3 us
  Pallas kernels  37.7 us (98%)
  other arithmetic  0.6 us (2%)
    pallas_call x1, Pallas kernels, body(): pl.pallas_call(kernel, out_shape=jax.ShapeDtypeStruct((8, 8, 256), F32),...  37.7 us

profile of v5, /device:TPU:1, one launch (start us, length us, event | category | flops | bytes accessed | tf_op | source)
XLA Modules:
  0.0 38.3 jit_solution(15219140667474834515)
XLA Ops:
  0.0 37.7 %shard_map.82 = f32[8,8,256]{2,1,0:T(8,128)S(1)} custom-call(s32[32]{0:T(128)} %lengths_in.1, bf16[1024,128]{1,0:T(8,128)(2,1)} %bitcast.9, bf16[32,32,64]{2,1,0:T(8,128)(2,1)} %q_rope.1, bf16[32,512,512]{2,1,0:T(8,128)(2,1)} %cache.1, bf16[32,64,512]{2,1,0:T(8,128)(2,1)} %bitcast.7, bf16[512,128]{1,0:T(8,128)(2,1)} %bitcast.10, bf16[32,512,128]{2,1,0:T(8,128)(2,1)} %w_uv.1, ...), custom_call_target="tpu_custom_call" | custom-call | tf_op jit(solution)/shard_map/pallas_call | solution.py:255
  37.7 0.6 %reduce_sum.9 = bf16[8,256]{1,0:T(8,128)(2,1)} reduce(f32[8,8,256]{2,1,0:T(8,128)S(1)} %shard_map.82, f32[]{:T(128)} %constant.0.clone.1), dimensions={0}, to_apply=%region_0.0 | reduce | flops 14336 | bytes 69636 | tf_op jit(solution)/shard_map/reduce_sum | solution.py:306

commit v6 on v5

--- a/solution.py
+++ b/solution.py
@@ -182,7 +182,7 @@
     for e in range(2):
         for k in range(4):
             lanes = slice(1024 * k, 1024 * k + 1024)
-            wot[lanes, 256 * e:256 * e + 256] = jnp.concatenate([wo[e, :, lanes], jnp.zeros((32, 1024), BF16)], axis=0).T
+            wot[k, :, 256 * e:256 * e + 256] = jnp.concatenate([wo[e, :, lanes], jnp.zeros((32, 1024), BF16)], axis=0).T
 
     arrived(statbuf, stat_sems.at[1])
     peaks, totals = statbuf[:, 0:4, :], statbuf[:, 4:8, :]
@@ -214,17 +214,17 @@
 
     for a, b in steps:
         device = (2 * (4 * ((z + a) % 4) + (y + b) % 4) + 1 - c, group)
-        remote(vmsg, vbuf.at[4 * y + x], v_sems.at[0], v_sems.at[1], device).start()
-    arrived(vbuf, v_sems.at[1])
+        remote(vmsg, vbuf.at[y, x], v_sems.at[4], v_sems.at[y], device).start()
     head_terms = jnp.zeros((16, 512), F32)
     for k in range(4):
-        vwide[k] = vbuf[4 * k:4 * k + 4].astype(F32).reshape(128, 128)
+        from_y = (y + k) % 4
+        arrived(vbuf.at[from_y], v_sems.at[from_y])
+        vwide[k] = vbuf[from_y].astype(F32).reshape(128, 128)
         for h in range(0, 8, 2):
             rows = jnp.concatenate(
                 [vwide[k, pl.ds(h, 16, stride=8), :], vwide[k, pl.ds(h + 1, 16, stride=8), :]], axis=1
             ).astype(BF16)
-            head = 8 * k + h
-            head_terms = head_terms + nn(rows, wot[128 * head:128 * head + 256, :])
+            head_terms = head_terms + nn(rows, wot[from_y, 128 * h:128 * h + 256, :])
 
     rows_c = lax.broadcasted_iota(jnp.int32, (8, 256), 0) // 4 == 1 - c
     for e in range(2):
@@ -245,7 +245,7 @@
         arrived(qbuf.at[i, pl.ds(0, 15)], q_sems.at[0, i])
         arrived(rsbuf.at[i, pl.ds(0, 15)], rs_sems.at[0, i])
     arrived(statbuf.at[pl.ds(0, 15)], stat_sems.at[0])
-    arrived(vbuf, v_sems.at[0])
+    arrived(vbuf, v_sems.at[4])
     arrived(terms.at[pl.ds(0, 7)], t_sems.at[0])
 
 
@@ -271,17 +271,17 @@
             pltpu.VMEM((2, 4, 512, 128), BF16),
             pltpu.VMEM((2, 224, 4096), BF16),
             pltpu.VMEM((4, 512, 1024), BF16),
-            pltpu.VMEM((4096, 512), BF16),
+            pltpu.VMEM((4, 1024, 512), BF16),
             pltpu.VMEM((4, 16, 16, 256), BF16),
             pltpu.VMEM((8, 128), F32),
             pltpu.VMEM((4, 16, 16, 256), BF16),
             pltpu.VMEM((16, 8, 128), F32),
             pltpu.VMEM((128, 128), F32),
             pltpu.VMEM((32, 128), BF16),
-            pltpu.VMEM((16, 32, 128), BF16),
+            pltpu.VMEM((4, 4, 32, 128), BF16),
             pltpu.VMEM((4, 128, 128), F32),
             pltpu.VMEM((8, 8, 256), F32),
-            dma((8,)), dma((2, 3)), dma((2, 3)), dma((2,)), dma((2, 4)), dma((2, 4)), dma((2,)), dma((2,)), dma((2,)), dma((4,)),
+            dma((8,)), dma((2, 3)), dma((2, 3)), dma((2,)), dma((2, 4)), dma((2, 4)), dma((2,)), dma((5,)), dma((2,)), dma((4,)),
             pltpu.SemaphoreType.REGULAR,
             pltpu.SMEM((32,), jnp.int32),
         ],

time: 38.4 us -> 38.1 us (level)
  no operation moved by 1% of the time
where the time goes in v6:
time: 38.1 us; the launch traced here: 38 us
  Pallas kernels  37.4 us (98%)
  other arithmetic  0.6 us (2%)
    pallas_call x1, Pallas kernels, body(): pl.pallas_call(kernel, out_shape=jax.ShapeDtypeStruct((8, 8, 256), F32),...  37.4 us

profile of v6, /device:TPU:1, one launch (start us, length us, event | category | flops | bytes accessed | tf_op | source)
XLA Modules:
  0.0 38.0 jit_solution(15026671474546220334)
XLA Ops:
  0.0 37.4 %shard_map.82 = f32[8,8,256]{2,1,0:T(8,128)S(1)} custom-call(s32[32]{0:T(128)} %lengths_in.1, bf16[1024,128]{1,0:T(8,128)(2,1)} %bitcast.9, bf16[32,32,64]{2,1,0:T(8,128)(2,1)} %q_rope.1, bf16[32,512,512]{2,1,0:T(8,128)(2,1)} %cache.1, bf16[32,64,512]{2,1,0:T(8,128)(2,1)} %bitcast.7, bf16[512,128]{1,0:T(8,128)(2,1)} %bitcast.10, bf16[32,512,128]{2,1,0:T(8,128)(2,1)} %w_uv.1, ...), custom_call_target="tpu_custom_call" | custom-call | tf_op jit(solution)/shard_map/pallas_call | solution.py:255
  37.4 0.6 %reduce_sum.9 = bf16[8,256]{1,0:T(8,128)(2,1)} reduce(f32[8,8,256]{2,1,0:T(8,128)S(1)} %shard_map.82, f32[]{:T(128)} %constant.0.clone.1), dimensions={0}, to_apply=%region_0.0 | reduce | flops 14336 | bytes 69636 | tf_op jit(solution)/shard_map/reduce_sum | solution.py:306

commit v7 on v6

--- a/solution.py
+++ b/solution.py
@@ -32,7 +32,8 @@
     z, y = chip // 4, chip % 4
     twin = ctx + 1 - 2 * c
     scale = (128 + 64) ** (-0.5)
-    group = (x + z) % 4
+    shift = (z + 2 * c) % 4
+    group = (x + shift) % 4
 
     def remote(src, dst, send_sem, recv_sem, device):
         return pltpu.make_async_remote_copy(
@@ -112,12 +113,11 @@
     ]
     twin_copies[0].start()
     twin_copies[1].start()
-    heads = w_uv.at[pl.ds(8 * y + 4 * c, 4)]
-    uv_local = pltpu.make_async_copy(heads, uv.at[c], uv_sems.at[1])
-    uv_push = remote(heads, uv.at[c], uv_sems.at[0], uv_sems.at[1], (ctx, (x + 4 - z) % 4))
-    pl.when(z == 0)(uv_local.start)
-    pl.when(z != 0)(uv_push.start)
-    uv_twin = remote(uv.at[c], uv.at[c], uv_sems.at[2], uv_sems.at[3], (twin, x))
+    heads = w_uv.at[pl.ds(8 * y, 8)]
+    uv_local = pltpu.make_async_copy(heads, uv, uv_sems.at[1])
+    uv_push = remote(heads, uv, uv_sems.at[0], uv_sems.at[1], (ctx, (x + 4 - shift) % 4))
+    pl.when(shift == 0)(uv_local.start)
+    pl.when(shift != 0)(uv_push.start)
 
     arrived(xbuf, x_sems.at[1])
     for i in range(4):
@@ -169,14 +169,12 @@
         obuf[i] = jnp.concatenate([part[:, :, 0:256], part[:, :, 256:512]], axis=1).astype(BF16)
         for a, b in steps:
             to_z, to_y = (z + a) % 4, (y + b) % 4
-            source = obuf.at[i, 4 * ((x + to_z) % 4) + to_y]
+            source = obuf.at[i, 4 * ((x + to_z + 2 * c) % 4) + to_y]
             if (a, b) == (0, 0):
                 pltpu.make_async_copy(source, rsbuf.at[i, chip], rs_sems.at[1, i]).start()
             else:
                 device = (2 * (4 * to_z + to_y) + c, x)
                 remote(source, rsbuf.at[i, chip], rs_sems.at[0, i], rs_sems.at[1, i], device).start()
-    uv_local.wait()
-    uv_twin.start()
     load_out.wait()
     twin_copies[2].wait_recv()
     for e in range(2):
@@ -203,11 +201,11 @@
     high = summed.astype(BF16)
     low = (summed - high.astype(F32)).astype(BF16)
     both = jnp.concatenate([high, low], axis=0)
-    uv_twin.wait_recv()
+    uv_local.wait()
     own_row = lax.broadcasted_iota(jnp.int32, (32, 128), 0) % 8
     values = jnp.zeros((32, 128), F32)
     for h in range(0, 8, 2):
-        product = nn(both, jnp.concatenate([uv[h // 4, h % 4], uv[h // 4, h % 4 + 1]], axis=1))
+        product = nn(both, jnp.concatenate([uv[h], uv[h + 1]], axis=1))
         product = product[0:32] + product[32:64]
         values = jnp.where(own_row == h, product[:, 0:128], jnp.where(own_row == h + 1, product[:, 128:256], values))
     vmsg[...] = values.astype(BF16)
@@ -237,9 +235,9 @@
     pltpu.make_async_copy(terms.at[slot], out.at[t_slot], t_sems.at[1]).start()
     arrived(out, t_sems.at[1])
 
-    for copy in rope_copies + twin_copies + [uv_twin]:
+    for copy in rope_copies + twin_copies:
         copy.wait_send()
-    pl.when(z != 0)(uv_push.wait_send)
+    pl.when(shift != 0)(uv_push.wait_send)
     arrived(ybuf.at[pl.ds(0, 7)], x_sems.at[0])
     for i in range(4):
         arrived(qbuf.at[i, pl.ds(0, 15)], q_sems.at[0, i])
@@ -268,7 +266,7 @@
             pltpu.VMEM((4, 128, 1024), F32),
             pltpu.VMEM((4, 1024, 512), BF16),
             pltpu.VMEM((4, 64, 1024), BF16),
-            pltpu.VMEM((2, 4, 512, 128), BF16),
+            pltpu.VMEM((8, 512, 128), BF16),
             pltpu.VMEM((2, 224, 4096), BF16),
             pltpu.VMEM((4, 512, 1024), BF16),
             pltpu.VMEM((4, 1024, 512), BF16),
@@ -281,7 +279,7 @@
             pltpu.VMEM((4, 4, 32, 128), BF16),
             pltpu.VMEM((4, 128, 128), F32),
             pltpu.VMEM((8, 8, 256), F32),
-            dma((8,)), dma((2, 3)), dma((2, 3)), dma((2,)), dma((2, 4)), dma((2, 4)), dma((2,)), dma((5,)), dma((2,)), dma((4,)),
+            dma((8,)), dma((2, 3)), dma((2, 3)), dma((2,)), dma((2, 4)), dma((2, 4)), dma((2,)), dma((5,)), dma((2,)), dma((2,)),
             pltpu.SemaphoreType.REGULAR,
             pltpu.SMEM((32,), jnp.int32),
         ],

time: 38.1 us -> 38 us (level)
  no operation moved by 1% of the time
where the time goes in v7:
time: 38 us; the launch traced here: 37.9 us
  Pallas kernels  37.3 us (98%)
  other arithmetic  0.6 us (2%)
    pallas_call x1, Pallas kernels, body(): pl.pallas_call(kernel, out_shape=jax.ShapeDtypeStruct((8, 8, 256), F32),...  37.3 us

profile of v7, /device:TPU:1, one launch (start us, length us, event | category | flops | bytes accessed | tf_op | source)
XLA Modules:
  0.0 37.9 jit_solution(18374572744200509476)
XLA Ops:
  0.0 37.3 %shard_map.82 = f32[8,8,256]{2,1,0:T(8,128)S(1)} custom-call(s32[32]{0:T(128)} %lengths_in.1, bf16[1024,128]{1,0:T(8,128)(2,1)} %bitcast.9, bf16[32,32,64]{2,1,0:T(8,128)(2,1)} %q_rope.1, bf16[32,512,512]{2,1,0:T(8,128)(2,1)} %cache.1, bf16[32,64,512]{2,1,0:T(8,128)(2,1)} %bitcast.7, bf16[512,128]{1,0:T(8,128)(2,1)} %bitcast.10, bf16[32,512,128]{2,1,0:T(8,128)(2,1)} %w_uv.1, ...), custom_call_target="tpu_custom_call" | custom-call | tf_op jit(solution)/shard_map/pallas_call | solution.py:253
  37.3 0.6 %reduce_sum.9 = bf16[8,256]{1,0:T(8,128)(2,1)} reduce(f32[8,8,256]{2,1,0:T(8,128)S(1)} %shard_map.82, f32[]{:T(128)} %constant.0.clone.1), dimensions={0}, to_apply=%region_0.0 | reduce | flops 14336 | bytes 69636 | tf_op jit(solution)/shard_map/reduce_sum | solution.py:304

commit v8 on v7

--- a/solution.py
+++ b/solution.py
@@ -120,11 +120,10 @@
     pl.when(shift != 0)(uv_push.start)
 
     arrived(xbuf, x_sems.at[1])
+    pl.semaphore_wait(ready, 3)
     for i in range(4):
         for e in range(2):
             ebuf[i, e] = jnp.concatenate([xbuf[2 * g + e, :, 32 * i:32 * i + 32] for g in range(4)], axis=1)
-    pl.semaphore_wait(ready, 3)
-    for i in range(4):
         for device in plane:
             remote(ebuf.at[i], qbuf.at[i, chip], q_sems.at[0, i], q_sems.at[1, i], device).start()
         pltpu.make_async_copy(ebuf.at[i], qbuf.at[i, chip], q_sems.at[1, i]).start()
@@ -152,15 +151,13 @@
 
     lane = lax.broadcasted_iota(jnp.int32, (128, 128), 1)
     stats = jnp.zeros((128, 128), F32)
-    scores = scores_of(0)
-    for i in range(4):
+    for i in range(4):
+        scores = scores_of(i)
         peak = jnp.maximum(jnp.max(scores, axis=1, keepdims=True), -1e29)
         weights = jnp.exp2((scores - peak) * (scale * 1.4426950408889634))
         total = jnp.sum(weights, axis=1, keepdims=True)
         stats = jnp.where(lane == i, peak, jnp.where(lane == 4 + i, total, stats))
-        if i < 3:
-            scores = scores_of(i + 1)
-        else:
+        if i == 3:
             stat[...] = stats.T[0:8, :]
             for device in plane:
                 remote(stat, statbuf.at[chip], stat_sems.at[0], stat_sems.at[1], device).start()

time: 38 us -> 37.2 us (0.979)
  Pallas kernels: 37.3 us -> 36.4 us
    pallas_call x1, Pallas kernels: 37.3 us -> 36.4 us  [body(): pl.pallas_call(kernel, out_shape=jax.ShapeDtypeStruct((8, 8, 256), F32),...]
where the time goes in v8:
time: 37.2 us; the launch traced here: 37.1 us
  Pallas kernels  36.4 us (98%)
  other arithmetic  0.6 us (2%)
    pallas_call x1, Pallas kernels, body(): pl.pallas_call(kernel, out_shape=jax.ShapeDtypeStruct((8, 8, 256), F32),...  36.4 us

profile of v8, /device:TPU:1, one launch (start us, length us, event | category | flops | bytes accessed | tf_op | source)
XLA Modules:
  0.0 37.1 jit_solution(9975705051648863033)
XLA Ops:
  0.0 36.4 %shard_map.82 = f32[8,8,256]{2,1,0:T(8,128)S(1)} custom-call(s32[32]{0:T(128)} %lengths_in.1, bf16[1024,128]{1,0:T(8,128)(2,1)} %bitcast.9, bf16[32,32,64]{2,1,0:T(8,128)(2,1)} %q_rope.1, bf16[32,512,512]{2,1,0:T(8,128)(2,1)} %cache.1, bf16[32,64,512]{2,1,0:T(8,128)(2,1)} %bitcast.7, bf16[512,128]{1,0:T(8,128)(2,1)} %bitcast.10, bf16[32,512,128]{2,1,0:T(8,128)(2,1)} %w_uv.1, ...), custom_call_target="tpu_custom_call" | custom-call | tf_op jit(solution)/shard_map/pallas_call | solution.py:250
  36.5 0.6 %reduce_sum.9 = bf16[8,256]{1,0:T(8,128)(2,1)} reduce(f32[8,8,256]{2,1,0:T(8,128)S(1)} %shard_map.82, f32[]{:T(128)} %constant.0.clone.1), dimensions={0}, to_apply=%region_0.0 | reduce | flops 14336 | bytes 69636 | tf_op jit(solution)/shard_map/reduce_sum | solution.py:301

commit v9 on v8

--- a/solution.py
+++ b/solution.py
@@ -44,7 +44,7 @@
         pltpu.make_async_copy(ref, ref, sem).wait()
 
     across = []
-    for k in range(1, 8):
+    for k in (4, 5, 2, 3, 6, 7, 1):
         to_x, to_c = (x + k // 2) % 4, (c + k) % 2
         across.append((to_x, to_c, (2 * chip + to_c, to_x)))
     steps = [(a, b) for a in range(4) for b in range(4)]
@@ -230,8 +230,6 @@
     for to_x, to_c, device in across:
         remote(terms.at[2 * to_x + to_c], out.at[t_slot], t_sems.at[0], t_sems.at[1], device).start()
     pltpu.make_async_copy(terms.at[slot], out.at[t_slot], t_sems.at[1]).start()
-    arrived(out, t_sems.at[1])
-
     for copy in rope_copies + twin_copies:
         copy.wait_send()
     pl.when(shift != 0)(uv_push.wait_send)
@@ -242,6 +240,7 @@
     arrived(statbuf.at[pl.ds(0, 15)], stat_sems.at[0])
     arrived(vbuf, v_sems.at[4])
     arrived(terms.at[pl.ds(0, 7)], t_sems.at[0])
+    arrived(out, t_sems.at[1])
 
 
 def body(q_nope, q_rope, latent_cache, rope_keys, lengths, w_uk, w_uv, w_out):

time: 37.2 us -> 37 us (level)
  no operation moved by 1% of the time
where the time goes in v9:
time: 37 us; the launch traced here: 36.9 us
  Pallas kernels  36.2 us (98%)
  other arithmetic  0.6 us (2%)
    pallas_call x1, Pallas kernels, body(): pl.pallas_call(kernel, out_shape=jax.ShapeDtypeStruct((8, 8, 256), F32),...  36.2 us

profile of v9, /device:TPU:1, one launch (start us, length us, event | category | flops | bytes accessed | tf_op | source)
XLA Modules:
  0.0 36.9 jit_solution(8555407790208541187)
XLA Ops:
  0.0 36.2 %shard_map.82 = f32[8,8,256]{2,1,0:T(8,128)S(1)} custom-call(s32[32]{0:T(128)} %lengths_in.1, bf16[1024,128]{1,0:T(8,128)(2,1)} %bitcast.9, bf16[32,32,64]{2,1,0:T(8,128)(2,1)} %q_rope.1, bf16[32,512,512]{2,1,0:T(8,128)(2,1)} %cache.1, bf16[32,64,512]{2,1,0:T(8,128)(2,1)} %bitcast.7, bf16[512,128]{1,0:T(8,128)(2,1)} %bitcast.10, bf16[32,512,128]{2,1,0:T(8,128)(2,1)} %w_uv.1, ...), custom_call_target="tpu_custom_call" | custom-call | tf_op jit(solution)/shard_map/pallas_call | solution.py:249
  36.2 0.6 %reduce_sum.9 = bf16[8,256]{1,0:T(8,128)(2,1)} reduce(f32[8,8,256]{2,1,0:T(8,128)S(1)} %shard_map.82, f32[]{:T(128)} %constant.0.clone.1), dimensions={0}, to_apply=%region_0.0 | reduce | flops 14336 | bytes 69636 | tf_op jit(solution)/shard_map/reduce_sum | solution.py:300

commit v10 on v9

--- a/solution.py
+++ b/solution.py
@@ -214,7 +214,7 @@
     for k in range(4):
         from_y = (y + k) % 4
         arrived(vbuf.at[from_y], v_sems.at[from_y])
-        vwide[k] = vbuf[from_y].astype(F32).reshape(128, 128)
+        vwide[k, 0:128] = vbuf[from_y].astype(F32).reshape(128, 128)
         for h in range(0, 8, 2):
             rows = jnp.concatenate(
                 [vwide[k, pl.ds(h, 16, stride=8), :], vwide[k, pl.ds(h + 1, 16, stride=8), :]], axis=1
@@ -273,7 +273,7 @@
             pltpu.VMEM((128, 128), F32),
             pltpu.VMEM((32, 128), BF16),
             pltpu.VMEM((4, 4, 32, 128), BF16),
-            pltpu.VMEM((4, 128, 128), F32),
+            pltpu.VMEM((4, 136, 128), F32),
             pltpu.VMEM((8, 8, 256), F32),
             dma((8,)), dma((2, 3)), dma((2, 3)), dma((2,)), dma((2, 4)), dma((2, 4)), dma((2,)), dma((5,)), dma((2,)), dma((2,)),
             pltpu.SemaphoreType.REGULAR,

time: 37 us -> 37 us (level)
  no operation moved by 1% of the time
where the time goes in v10:
time: 37 us; the launch traced here: 36.9 us
  Pallas kernels  36.2 us (98%)
  other arithmetic  0.6 us (2%)
    pallas_call x1, Pallas kernels, body(): pl.pallas_call(kernel, out_shape=jax.ShapeDtypeStruct((8, 8, 256), F32),...  36.2 us

profile of v10, /device:TPU:1, one launch (start us, length us, event | category | flops | bytes accessed | tf_op | source)
XLA Modules:
  0.0 36.9 jit_solution(11269868735850763204)
XLA Ops:
  0.0 36.2 %shard_map.82 = f32[8,8,256]{2,1,0:T(8,128)S(1)} custom-call(s32[32]{0:T(128)} %lengths_in.1, bf16[1024,128]{1,0:T(8,128)(2,1)} %bitcast.9, bf16[32,32,64]{2,1,0:T(8,128)(2,1)} %q_rope.1, bf16[32,512,512]{2,1,0:T(8,128)(2,1)} %cache.1, bf16[32,64,512]{2,1,0:T(8,128)(2,1)} %bitcast.7, bf16[512,128]{1,0:T(8,128)(2,1)} %bitcast.10, bf16[32,512,128]{2,1,0:T(8,128)(2,1)} %w_uv.1, ...), custom_call_target="tpu_custom_call" | custom-call | tf_op jit(solution)/shard_map/pallas_call | solution.py:249
  36.2 0.6 %reduce_sum.9 = bf16[8,256]{1,0:T(8,128)(2,1)} reduce(f32[8,8,256]{2,1,0:T(8,128)S(1)} %shard_map.82, f32[]{:T(128)} %constant.0.clone.1), dimensions={0}, to_apply=%region_0.0 | reduce | flops 14336 | bytes 69636 | tf_op jit(solution)/shard_map/reduce_sum | solution.py:300
